TPU v7x, 32 devices: a whole 2x2x4 slice. The times are simulated.
32 devices in a mesh: dp: 4 (over y, x), expert: 4 (over z), tensor: 2 (over core).
Axes of the slice: x: 2, y: 2, z: 4, core: 2. Of those that a mesh axis runs over, the one named last changes fastest.
Arguments:
- tokens: bfloat16 [8192, 1536], P(('dp', 'expert')), may hold values from -6 to 6
- out_grad: bfloat16 [8192, 1536], P(('dp', 'expert')), may hold values from -6 to 6
- attn_gain: float32 [1536], replicated, may hold values from 0.5 to 1.5
- query_weight: bfloat16 [1536, 1536], P(None, 'tensor'), may hold values from -0.625 to 0.625
- key_value_weight: bfloat16 [2, 1536, 512], P(None, None, 'tensor'), may hold values from -0.625 to 0.625
- output_weight: bfloat16 [1536, 1536], P('tensor'), may hold values from -0.625 to 0.625
- expert_gain: float32 [1536], replicated, may hold values from 0.5 to 1.5
- router_weight: bfloat16 [1536, 20], replicated, may hold values from -0.078125 to 0.078125
- gateup_weight: bfloat16 [20, 2, 1536, 512], P('expert', None, None, 'tensor'), may hold values from -0.15625 to 0.15625
- down_weight: bfloat16 [20, 512, 1536], P('expert', 'tensor'), may hold values from -4 to 4
- routes: int32 [8192, 8], P(('dp', 'expert')), may hold values from 0 to 19, all different within a row; in each aligned block of 512 rows (0 to 511, 512 to 1023, ...) at most 256 rows name the same one
Outputs:
- mixed: bfloat16 [8192, 1536], P(('dp', 'expert'))
- tokens_grad: float32 [8192, 1536], P(('dp', 'expert'))
- attn_gain_grad: float32 [1536], P(('dp', 'expert'))
- query_grad: float32 [1536, 1536], P(('dp', 'expert'), 'tensor')
- keyvalue_grad: float32 [2, 1536, 512], P(None, ('dp', 'expert'), 'tensor')
- output_weight_grad: float32 [1536, 1536], P('tensor', ('dp', 'expert'))
- expert_gain_grad: float32 [1536], P(('dp', 'expert'))
- router_grad: float32 [1536, 20], P(('dp', 'expert'))
- gateup_grad: float32 [20, 2, 1536, 512], P('expert', None, 'dp', 'tensor')
- down_grad: float32 [20, 512, 1536], P('expert', 'tensor', 'dp')
Inputs may be any that keep to these rules, and one draw needn't show every extreme that they name: `routes`: each row names 8 different experts. Within each aligned block of 512 rows no expert is named by more than 256 rows, a bound that some block reaches.
All inputs are finite; a program needn't handle non-finite values.
Results may differ from a plain program's by a relative error of at most 0.018.
The roundings to bfloat16 on the way count: a program that leaves them out, or rounds other values in their place, can miss the bound.
Values may be sent and summed in bfloat16 or wider, within the bound.
A program may use at most 320 MiB of HBM per device.

v0:
```python
import jax
import jax.numpy as jnp
from jax import lax
from jax.sharding import PartitionSpec as P

HEAD_SIZE = 64
TOPK = 8
SEQUENCE_LENGTH = 512


EPSILON = 1e-06
RESIDUAL = 0.22
ATTN_SCALE = 0.015625
ROPE_BASE = 10000.0
NEGATIVE = -1e30


def rotary_tables(length):
    half_dim = HEAD_SIZE // 2
    frequency = ROPE_BASE ** (-jnp.arange(half_dim, dtype=jnp.float32) * 2.0 / HEAD_SIZE)
    angles = jnp.arange(length, dtype=jnp.float32)[:, None] * frequency[None, :]
    return (jnp.cos(angles)[:, None, :], jnp.sin(angles)[:, None, :])


def rotate(value_rows, cosine, sine_table):
    half_dim = value_rows.shape[-1] // 2
    first = value_rows[..., :half_dim]
    second = value_rows[..., half_dim:]
    return jnp.concatenate(
        [first * cosine - second * sine_table, second * cosine + first * sine_table], axis=-1
    )


def rotate_back(grads, cosine, sine_table):
    half_dim = grads.shape[-1] // 2
    first = grads[..., :half_dim]
    second = grads[..., half_dim:]
    return jnp.concatenate(
        [first * cosine + second * sine_table, second * cosine - first * sine_table], axis=-1
    )


def norm_forward(value_rows):
    inv_rms = lax.rsqrt(jnp.mean(value_rows * value_rows, axis=-1, keepdims=True) + EPSILON)
    return (value_rows * inv_rms, inv_rms)


def norm_backward(grad_normed, gain, normal_unit, inv_rms):
    grad_unit = grad_normed * gain
    grad_input = inv_rms * (
        grad_unit - normal_unit * jnp.mean(grad_unit * normal_unit, axis=-1, keepdims=True)
    )
    return (grad_input, jnp.sum(grad_normed * normal_unit, axis=0))


def block_scores(query_block, key_block, row_start):
    scores = (
        jnp.einsum("sqjgd,skjd->sjgqk", query_block, key_block, preferred_element_type=jnp.float32)
        * ATTN_SCALE
    )
    row_ids = row_start + jnp.arange(query_block.shape[1])[:, None]
    col_ids = jnp.arange(key_block.shape[1])[None, :]
    return jnp.where(row_ids >= col_ids, scores, NEGATIVE)


def per_device(
    tokens,
    out_grad,
    attn_gain,
    query_weight,
    key_value_weight,
    output_weight,
    expert_gain,
    router_weight,
    gateup_weight,
    down_weight,
    routes,
):
    tok_count = tokens.shape[0]
    feat_width = tokens.shape[1]
    expert_count = router_weight.shape[1]
    owner_count = lax.axis_size("expert")
    local_experts = gateup_weight.shape[0]
    capacity = tok_count * TOPK * 5 // (4 * expert_count) // 2 * 2
    kv_heads = key_value_weight.shape[2] // HEAD_SIZE
    query_heads = query_weight.shape[1] // HEAD_SIZE
    groups = query_heads // kv_heads
    sequence_count = tok_count // SEQUENCE_LENGTH
    block_rows = min(512, SEQUENCE_LENGTH)
    pair_count = tok_count * TOPK
    cosine, sine_table = rotary_tables(SEQUENCE_LENGTH)
    inputs = tokens.astype(jnp.float32)
    unit_first, rms_first = norm_forward(inputs)
    normed = (unit_first * attn_gain).astype(jnp.bfloat16)
    queries = jnp.dot(normed, query_weight, preferred_element_type=jnp.float32)
    key_value = jnp.einsum(
        "td,cde->cte", normed, key_value_weight, preferred_element_type=jnp.float32
    )
    query_rot = (
        rotate(
            queries.reshape(sequence_count, SEQUENCE_LENGTH, query_heads, HEAD_SIZE),
            cosine,
            sine_table,
        )
        .astype(jnp.bfloat16)
        .reshape(sequence_count, SEQUENCE_LENGTH, kv_heads, groups, HEAD_SIZE)
    )
    keys_rot = rotate(
        key_value[0].reshape(sequence_count, SEQUENCE_LENGTH, kv_heads, HEAD_SIZE),
        cosine,
        sine_table,
    ).astype(jnp.bfloat16)
    value_rows = (
        key_value[1]
        .astype(jnp.bfloat16)
        .reshape(sequence_count, SEQUENCE_LENGTH, kv_heads, HEAD_SIZE)
    )
    row_start = 0
    scores = block_scores(query_rot, keys_rot, row_start)
    row_max = jnp.max(scores, axis=-1, keepdims=True)
    exp_scores = jnp.exp(scores - row_max)
    row_sum = jnp.sum(exp_scores, axis=-1, keepdims=True)
    prob_block = (exp_scores / row_sum).astype(jnp.bfloat16)
    outputs = jnp.einsum(
        "sjgqk,skjd->sqjgd", prob_block, value_rows, preferred_element_type=jnp.float32
    )
    heads_out = outputs.astype(jnp.bfloat16).reshape(tok_count, query_heads * HEAD_SIZE)
    partial_value = jnp.dot(heads_out, output_weight, preferred_element_type=jnp.float32)
    attention = lax.psum(partial_value, "tensor")
    middle = inputs + RESIDUAL * attention
    unit_second, rms_second = norm_forward(middle)
    expert_in = (unit_second * expert_gain).astype(jnp.bfloat16)
    logits = jnp.dot(expert_in, router_weight, preferred_element_type=jnp.float32)
    pick_mask = (
        routes[:, :, None] == jnp.arange(expert_count, dtype=jnp.int32)[None, None, :]
    ).astype(jnp.float32)
    chosen = jnp.sum(pick_mask * logits[:, None, :], axis=-1)
    gates = jax.nn.softmax(chosen, axis=-1)
    pair_expert = routes.reshape(pair_count)
    hit_table = (pair_expert[:, None] == jnp.arange(expert_count, dtype=jnp.int32)[None, :]).astype(
        jnp.int32
    )
    slot_place = jnp.sum((jnp.cumsum(hit_table, axis=0) - hit_table) * hit_table, axis=1)
    slot_pair = (
        jnp.full((expert_count, capacity), pair_count, jnp.int32)
        .at[pair_expert, slot_place]
        .set(jnp.arange(pair_count, dtype=jnp.int32))
    )
    slot_token = slot_pair // TOPK
    pair_slot = pair_expert * capacity + slot_place
    gateup_use, down_use = (gateup_weight, down_weight)
    padded_in = jnp.concatenate([expert_in, jnp.zeros((1, feat_width), jnp.bfloat16)], axis=0)
    buffer = padded_in[slot_token]
    arrived = lax.all_to_all(
        buffer.reshape(expert_count, 1, buffer.shape[1], feat_width),
        "expert",
        split_axis=0,
        concat_axis=1,
        tiled=True,
    )
    slot_cols = arrived.shape[2]
    expert_rows = arrived.reshape(local_experts, owner_count * slot_cols, feat_width)
    hidden = jnp.einsum(
        "erd,ecdf->ercf", expert_rows, gateup_use, preferred_element_type=jnp.float32
    )
    gate_part = hidden[:, :, 0]
    up_part = hidden[:, :, 1]
    sigmoid_gate = jax.nn.sigmoid(gate_part)
    silu_gate = gate_part * sigmoid_gate
    activation = (silu_gate * up_part).astype(jnp.bfloat16)
    partial_out = jnp.einsum(
        "erf,efd->erd", activation, down_use, preferred_element_type=jnp.float32
    )
    summed = lax.psum_scatter(
        partial_out.reshape(local_experts, owner_count, capacity, feat_width),
        "tensor",
        scatter_dimension=2,
        tiled=True,
    )
    back_rows = lax.all_to_all(
        summed.astype(jnp.bfloat16), "expert", split_axis=1, concat_axis=0, tiled=True
    )
    returned = lax.all_gather(back_rows, "tensor", axis=2, tiled=True).reshape(
        expert_count * capacity, feat_width
    )
    pair_rows = returned[pair_slot].reshape(tok_count, TOPK, feat_width)
    combined = jnp.sum(gates[:, :, None] * pair_rows, axis=1)
    output = (middle + RESIDUAL * combined).astype(jnp.bfloat16)
    grad_out = out_grad.astype(jnp.float32)
    grad_gate = RESIDUAL * jnp.einsum(
        "td,tkd->tk", out_grad, pair_rows, preferred_element_type=jnp.float32
    )
    grad_chosen = gates * (grad_gate - jnp.sum(gates * grad_gate, axis=-1, keepdims=True))
    grad_logits = jnp.sum(pick_mask * grad_chosen[:, :, None], axis=1).astype(jnp.bfloat16)
    grad_pairs = (
        (RESIDUAL * gates[:, :, None] * grad_out[:, None, :])
        .astype(jnp.bfloat16)
        .reshape(pair_count, feat_width)
    )
    grad_buffer = jnp.concatenate([grad_pairs, jnp.zeros((1, feat_width), jnp.bfloat16)], axis=0)[
        slot_pair
    ]
    grad_arrived = lax.all_to_all(
        grad_buffer.reshape(expert_count, 1, grad_buffer.shape[1], feat_width),
        "expert",
        split_axis=0,
        concat_axis=1,
        tiled=True,
    )
    grad_rows = grad_arrived.reshape(local_experts, owner_count * slot_cols, feat_width)
    grad_act = jnp.einsum("erd,efd->erf", grad_rows, down_use, preferred_element_type=jnp.float32)
    down_grad = jnp.einsum(
        "erf,erd->efd", activation, grad_rows, preferred_element_type=jnp.float32
    )
    grad_gatepart = grad_act * up_part * sigmoid_gate * (1.0 + gate_part * (1.0 - sigmoid_gate))
    grad_uppart = grad_act * silu_gate
    grad_hidden = jnp.stack([grad_gatepart, grad_uppart], axis=2).astype(jnp.bfloat16)
    gateup_grad = jnp.einsum(
        "erd,ercf->ecdf", expert_rows, grad_hidden, preferred_element_type=jnp.float32
    )
    grad_rows_in = jnp.einsum(
        "ercf,ecdf->erd", grad_hidden, gateup_use, preferred_element_type=jnp.float32
    )
    grad_summed = lax.psum_scatter(
        grad_rows_in.reshape(local_experts, owner_count, capacity, feat_width),
        "tensor",
        scatter_dimension=2,
        tiled=True,
    )
    grad_back = lax.all_to_all(
        grad_summed.astype(jnp.bfloat16), "expert", split_axis=1, concat_axis=0, tiled=True
    )
    grad_returned = lax.all_gather(grad_back, "tensor", axis=2, tiled=True).reshape(
        expert_count * capacity, feat_width
    )
    grad_expert_in = jnp.sum(
        grad_returned[pair_slot].reshape(tok_count, TOPK, feat_width), axis=1, dtype=jnp.float32
    )
    grad_expert_in = grad_expert_in + jnp.einsum(
        "te,de->td", grad_logits, router_weight, preferred_element_type=jnp.float32
    )
    router_grad = jnp.einsum(
        "td,te->de", expert_in, grad_logits, preferred_element_type=jnp.float32
    )
    grad_middle_norm, expert_gain_grad = norm_backward(
        grad_expert_in, expert_gain, unit_second, rms_second
    )
    grad_middle = grad_out + grad_middle_norm
    grad_attn = (RESIDUAL * grad_middle).astype(jnp.bfloat16)
    output_weight_grad = jnp.einsum(
        "te,td->ed", heads_out, grad_attn, preferred_element_type=jnp.float32
    )
    grad_heads = (
        jnp.einsum("td,ed->te", grad_attn, output_weight, preferred_element_type=jnp.float32)
        .astype(jnp.bfloat16)
        .reshape(sequence_count, SEQUENCE_LENGTH, kv_heads, groups, HEAD_SIZE)
    )
    grad_keys = jnp.zeros((sequence_count, SEQUENCE_LENGTH, kv_heads, HEAD_SIZE), jnp.float32)
    grad_values = jnp.zeros((sequence_count, SEQUENCE_LENGTH, kv_heads, HEAD_SIZE), jnp.float32)
    row_start = 0
    row_stop = row_start + block_rows
    scores = block_scores(query_rot, keys_rot, row_start)
    prob_block = jnp.exp(scores - row_max) / row_sum
    grad_probs = jnp.einsum(
        "sqjgd,skjd->sjgqk", grad_heads, value_rows, preferred_element_type=jnp.float32
    )
    grad_values = grad_values.at[:, :row_stop].add(
        jnp.einsum(
            "sjgqk,sqjgd->skjd",
            prob_block.astype(jnp.bfloat16),
            grad_heads,
            preferred_element_type=jnp.float32,
        )
    )
    grad_scores = (
        prob_block * (grad_probs - jnp.sum(prob_block * grad_probs, axis=-1, keepdims=True))
    ).astype(jnp.bfloat16)
    grad_queries = (
        jnp.einsum("sjgqk,skjd->sqjgd", grad_scores, keys_rot, preferred_element_type=jnp.float32)
        * ATTN_SCALE
    )
    grad_keys = grad_keys.at[:, :row_stop].add(
        jnp.einsum("sjgqk,sqjgd->skjd", grad_scores, query_rot, preferred_element_type=jnp.float32)
        * ATTN_SCALE
    )
    grad_query = (
        rotate_back(
            grad_queries.reshape(sequence_count, SEQUENCE_LENGTH, query_heads, HEAD_SIZE),
            cosine,
            sine_table,
        )
        .astype(jnp.bfloat16)
        .reshape(tok_count, query_heads * HEAD_SIZE)
    )
    grad_key = (
        rotate_back(grad_keys, cosine, sine_table)
        .astype(jnp.bfloat16)
        .reshape(tok_count, kv_heads * HEAD_SIZE)
    )
    grad_value = grad_values.astype(jnp.bfloat16).reshape(tok_count, kv_heads * HEAD_SIZE)
    grad_keyval = jnp.stack([grad_key, grad_value], axis=0)
    query_grad = jnp.einsum("td,te->de", normed, grad_query, preferred_element_type=jnp.float32)
    keyvalue_grad = jnp.einsum(
        "td,cte->cde", normed, grad_keyval, preferred_element_type=jnp.float32
    )
    grad_normed = jnp.einsum(
        "te,de->td", grad_query, query_weight, preferred_element_type=jnp.float32
    )
    grad_normed = grad_normed + jnp.einsum(
        "cte,cde->td", grad_keyval, key_value_weight, preferred_element_type=jnp.float32
    )
    grad_normed = lax.psum(grad_normed.astype(jnp.bfloat16), "tensor").astype(jnp.float32)
    grad_first, attn_gain_grad = norm_backward(grad_normed, attn_gain, unit_first, rms_first)
    tokens_grad = grad_middle + grad_first
    shared = (
        lax.psum_scatter(attn_gain_grad, ("dp", "expert"), scatter_dimension=0, tiled=True),
        lax.psum_scatter(query_grad, ("dp", "expert"), scatter_dimension=0, tiled=True),
        lax.psum_scatter(keyvalue_grad, ("dp", "expert"), scatter_dimension=1, tiled=True),
        lax.psum_scatter(output_weight_grad, ("dp", "expert"), scatter_dimension=1, tiled=True),
        lax.psum_scatter(expert_gain_grad, ("dp", "expert"), scatter_dimension=0, tiled=True),
        lax.psum_scatter(router_grad, ("dp", "expert"), scatter_dimension=0, tiled=True),
    )
    gateup_total, down_total = (
        lax.psum_scatter(
            gateup_grad.astype(jnp.bfloat16), "dp", scatter_dimension=2, tiled=True
        ).astype(jnp.float32),
        lax.psum_scatter(
            down_grad.astype(jnp.bfloat16), "dp", scatter_dimension=2, tiled=True
        ).astype(jnp.float32),
    )
    return (
        output,
        tokens_grad,
        shared[0],
        shared[1],
        shared[2],
        shared[3],
        shared[4],
        shared[5],
        gateup_total,
        down_total,
    )


def solution(mesh):
    placed = (
        P(("dp", "expert"), None),
        P(("dp", "expert"), None),
        P(),
        P(None, "tensor"),
        P(None, None, "tensor"),
        P("tensor", None),
        P(),
        P(),
        P("expert", None, None, "tensor"),
        P("expert", "tensor", None),
        P(("dp", "expert"), None),
    )
    return jax.shard_map(
        per_device,
        mesh=mesh,
        in_specs=placed,
        out_specs=(
            P(("dp", "expert"), None),
            P(("dp", "expert"), None),
            P(("dp", "expert")),
            P(("dp", "expert"), "tensor"),
            P(None, ("dp", "expert"), "tensor"),
            P("tensor", ("dp", "expert")),
            P(("dp", "expert")),
            P(("dp", "expert"), None),
            P("expert", None, "dp", "tensor"),
            P("expert", "tensor", "dp"),
        ),
        check_vma=False,
    )
```

profile of v0, /device:TPU:0, one launch (start us, length us, event | category | flops | bytes accessed | tf_op | source)
XLA Modules:
  0.0 2259.9 jit_solution(10449603576962841457)
XLA Ops:
  37.9 15.5 scatter_custom_fusion
  62.6 33.0 %gather_fusion = bf16[5120,1536]{1,0:T(8,128)(2,1)} fusion(bf16[513,1536]{1,0:T(8,128)(2,1)} %concatenate.56, s32[5120]{0:T(1024)S(1)} %broadcast_clamp_fusion.1), kind=kCustom, calls=%fused_computation | custom fusion | bytes 31477760 | tf_op jit(solution)/shard_map/gather | solution.py:153
  95.6 345.7 %all_to_all.66 = bf16[20,1,256,1536]{3,2,1,0:T(8,128)(2,1)S(1)} all-to-all(bf16[20,1,256,1536]{3,2,1,0:T(8,128)(2,1)} %bitcast.251), channel_id=1, replica_groups=mesh['dp'=4,'expert'=4,'tensor'=2] {'expert'}, dimensions={0} | all-to-all | bytes 31457280 | tf_op jit(solution)/shard_map/all_to_all | solution.py:154
  443.7 16.0 fusion.87
  465.5 17.5 fusion.88
  483.1 22.1 copy.108
  505.2 42.0 %reduce-scatter.14.cloned.1.call-done = f32[5,4,128,1536]{3,2,0,1:T(8,128)} async-done(((f32[5,4,256,1536]{3,2,0,1:T(8,128)}), f32[5,4,128,1536]{3,2,0,1:T(8,128)}) %reduce-scatter.14.cloned.1.call-update) | async-done | bytes 15728656 | tf_op jit(solution)/shard_map/reduce_scatter | solution.py:174
  547.3 9.7 convert_element_type.152
  557.0 179.9 %all_to_all.67 = bf16[5,4,128,1536]{3,2,0,1:T(8,128)(2,1)} all-to-all(bf16[5,4,128,1536]{3,2,0,1:T(8,128)(2,1)} %convert_element_type.152), channel_id=1, replica_groups=mesh['dp'=4,'expert'=4,'tensor'=2] {'expert'}, dimensions={1} | all-to-all | bytes 15728640 | tf_op jit(solution)/shard_map/all_to_all | solution.py:180
  742.8 22.2 all-gather.3.cloned.1.call-done
  765.0 32.8 %gather_fusion.1 = bf16[4096,1536]{1,0:T(8,128)(2,1)} fusion(bf16[5120,1536]{1,0:T(8,128)(2,1)} %bitcast.249, s32[4096]{0:T(1024)S(1)} %broadcast_clamp_fusion.2), kind=kCustom, calls=%fused_computation.1 | custom fusion | bytes 25182208 | tf_op jit(solution)/shard_map/gather | solution.py:186
  818.5 37.5 %gather_fusion.2 = bf16[5120,1536]{1,0:T(8,128)(2,1)} fusion(bf16[4097,1536]{1,0:T(8,128)(2,1)} %concatenate.58, s32[5120]{0:T(1024)S(1)} %broadcast_clamp_fusion), kind=kCustom, calls=%fused_computation.2 | custom fusion | bytes 31477760 | tf_op jit(solution)/shard_map/gather | solution.py:200
  856.1 346.0 %all_to_all.68 = bf16[20,1,256,1536]{3,2,1,0:T(8,128)(2,1)S(1)} all-to-all(bf16[20,1,256,1536]{3,2,1,0:T(8,128)(2,1)} %bitcast.252), channel_id=1, replica_groups=mesh['dp'=4,'expert'=4,'tensor'=2] {'expert'}, dimensions={0} | all-to-all | bytes 31457280 | tf_op jit(solution)/shard_map/all_to_all | solution.py:203
  1208.9 12.8 fusion.33
  1221.7 18.2 fusion.9
  1239.9 22.1 copy.113
  1262.1 42.0 %reduce-scatter.16.cloned.1.call-done = f32[5,4,128,1536]{3,2,0,1:T(8,128)} async-done(((f32[5,4,256,1536]{3,2,0,1:T(8,128)}), f32[5,4,128,1536]{3,2,0,1:T(8,128)}) %reduce-scatter.16.cloned.1.call-update) | async-done | bytes 15728656 | tf_op jit(solution)/shard_map/reduce_scatter | solution.py:224
  1304.1 9.7 convert_element_type.157
  1313.8 180.0 %all_to_all.69 = bf16[5,4,128,1536]{3,2,0,1:T(8,128)(2,1)} all-to-all(bf16[5,4,128,1536]{3,2,0,1:T(8,128)(2,1)} %convert_element_type.157), channel_id=1, replica_groups=mesh['dp'=4,'expert'=4,'tensor'=2] {'expert'}, dimensions={1} | all-to-all | bytes 15728640 | tf_op jit(solution)/shard_map/all_to_all | solution.py:230
  1498.0 16.9 convolution_convert_fusion
  1529.8 15.5 convert_bitcast_fusion
  1545.4 20.0 copy.145
  1565.4 17.8 reshape.576
  1584.1 12.9 multiply_reduce_fusion
  1597.0 32.9 %gather_fusion.3 = bf16[4096,1536]{1,0:T(8,128)(2,1)} fusion(bf16[5120,1536]{1,0:T(8,128)(2,1)} %bitcast.248, s32[4096]{0:T(1024)S(1)} %copy-done.39), kind=kCustom, calls=%fused_computation.3 | custom fusion | bytes 25182208 | tf_op jit(solution)/shard_map/gather | solution.py:237
  1629.8 10.7 convert_reduce_fusion
  1650.7 11.3 fusion.1
  1726.9 64.0 %reduce-scatter.24.cloned.1.call-done = bf16[384,2560]{1,0:T(8,128)(2,1)} async-done(((bf16[1536,2560]{1,0:T(8,128)(2,1)}), bf16[384,2560]{1,0:T(8,128)(2,1)}) %reduce-scatter.24.cloned.1.call-update) | async-done | bytes 1966096
  1816.8 78.9 %all-reduce.5 = (f32[1536]{0:T(1024)S(1)}, f32[1536]{0:T(1024)S(1)}) all-reduce(f32[1536]{0:T(1024)S(1)} %get-tuple-element.92, f32[1536]{0:T(1024)S(1)} %get-tuple-element.90), channel_id=4, replica_groups=mesh['dp'=4,'expert'=4,'tensor'=2] {'dp','expert'}, use_global_device_ids=true, to_apply=%region_23.24.clone | all-reduce | flops 3072 | bytes 24576
  1902.4 66.1 %all-reduce.14.cloned.1.call-done = f32[2,1536,256]{2,0,1:T(2,128)} async-done(((f32[2,1536,256]{2,0,1:T(2,128)}), f32[2,1536,256]{2,0,1:T(2,128)}) %all-reduce.14.cloned.1.call-update) | async-done | bytes 3145744
  1970.1 140.6 %reduce-scatter.18.cloned.1.call-done = f32[96,768]{1,0:T(8,128)} async-done(((f32[1536,768]{1,0:T(8,128)}), f32[96,768]{1,0:T(8,128)}) %reduce-scatter.18.cloned.1.call-update) | async-done | bytes 294928 | tf_op jit(solution)/shard_map/reduce_scatter | solution.py:317
  2110.8 141.9 %reduce-scatter.20.cloned.1.call-done = f32[768,96]{0,1:T(8,128)} async-done(((f32[768,1536]{0,1:T(8,128)}), f32[768,96]{0,1:T(8,128)}) %reduce-scatter.20.cloned.1.call-update) | async-done | bytes 294928 | tf_op jit(solution)/shard_map/reduce_scatter | solution.py:319
  (250 shorter events, 209.1 us)
Async XLA Ops:
  7.2 18.9 copy-start
  7.2 48.1 %all-reduce.10.cloned.1.call-start = ((), (), s32[]{:S(2)}) async-start(), calls=%async_computation.11 | async-start | bytes 6291456 | tf_op jit(solution)/shard_map/psum | solution.py:129
  7.3 12.4 copy-start.14
  12.6 7.1 copy-start.33
  29.1 8.5 copy-start.53
  29.2 8.6 copy-start.52
  29.2 518.1 %reduce-scatter.14.cloned.1.call-start = ((), (), s32[]{:S(2)}) async-start(), calls=%async_computation.12 | async-start | bytes 47185920 | tf_op jit(solution)/shard_map/reduce_scatter | solution.py:174
  443.7 16.0 copy-start.8
  505.2 259.8 %all-gather.3.cloned.1.call-start = ((), (), s32[]{:S(2)}) async-start(), calls=%async_computation.13 | async-start | bytes 23592960 | tf_op jit(solution)/shard_map/all_gather | solution.py:183
  737.0 567.1 %reduce-scatter.16.cloned.1.call-start = ((), (), s32[]{:S(2)}) async-start(), calls=%async_computation.14 | async-start | bytes 47185920 | tf_op jit(solution)/shard_map/reduce_scatter | solution.py:224
  740.7 57.1 %copy-start.38 = (s32[4096]{0:T(1024)}, s32[4096]{0:T(1024)S(1)}, u32[]{:S(2)}) copy-start(s32[4096]{0:T(1024)S(1)} %broadcast_clamp_fusion.2) | copy-start | bytes 49156
  1262.0 334.9 %all-gather.5.cloned.1.call-start = ((), (), s32[]{:S(2)}) async-start(), calls=%async_computation.15 | async-start | bytes 23592960 | tf_op jit(solution)/shard_map/all_gather | solution.py:233
  1493.8 224.8 %reduce-scatter.22.cloned.1.call-start = ((), (), s32[]{:S(2)}) async-start(), calls=%async_computation.19 | async-start | bytes 835584
  1497.6 222.5 %reduce-scatter.26.cloned.1.call-start = ((), (), s32[]{:S(2)}) async-start(), calls=%async_computation.21 | async-start | bytes 4915200
  1529.8 261.2 %reduce-scatter.24.cloned.1.call-start = ((), (), s32[]{:S(2)}) async-start(), calls=%async_computation.20 | async-start | bytes 9830400
  1583.3 230.6 %all-reduce.12.cloned.1.call-start = ((), (), s32[]{:S(2)}) async-start(), calls=%async_computation.16 | async-start | bytes 3145728 | tf_op jit(solution)/shard_map/psum | solution.py:312
  1584.1 12.9 copy-start.39
  1629.8 10.7 copy-start.4
  1629.8 10.7 copy-start.32
  1629.8 10.7 copy-start.47
  1629.8 10.7 copy-start.51
  1650.6 11.4 copy-start.26
  1650.6 11.4 slice-start
  1650.7 11.4 slice-start.1
  1650.7 13.0 slice-start.2
  1663.7 7.3 copy-start.22
  1663.7 7.3 copy-start.24
  1673.9 11.1 copy-start.28
  1673.9 11.1 copy-start.30
  1694.5 274.0 %all-reduce.14.cloned.1.call-start = ((), (), s32[]{:S(2)}) async-start(), calls=%async_computation.22 | async-start | bytes 6291456
  1704.6 406.1 %reduce-scatter.18.cloned.1.call-start = ((), (), s32[]{:S(2)}) async-start(), calls=%async_computation.17 | async-start | bytes 5013504 | tf_op jit(solution)/shard_map/reduce_scatter | solution.py:317
  1710.1 542.5 %reduce-scatter.20.cloned.1.call-start = ((), (), s32[]{:S(2)}) async-start(), calls=%async_computation.18 | async-start | bytes 5013504 | tf_op jit(solution)/shard_map/reduce_scatter | solution.py:319
  (40 other events, 107.3 us)
Sparse Core Ops, SparseCore 0:
  29.3 25.9 all-reduce.9
  505.3 41.9 reduce-scatter.13
  737.1 27.8 all-gather.2
  1262.1 41.8 reduce-scatter.15
  1493.9 27.8 all-gather.4
  1527.1 123.5 reduce-scatter.21
  1654.7 49.6 reduce-scatter.25
  1707.6 83.3 reduce-scatter.23
  1793.4 20.3 all-reduce.11
  1819.3 149.1 all-reduce.13
  1975.0 135.6 reduce-scatter.17
  2116.4 136.2 reduce-scatter.19
where the time goes:
time: 2270 us; the launch traced here: 2260 us
  blocking collectives  1130 us (50%)
  waiting for transfers between devices  528 us (23%)
  local copies, waits for them, and re-layouts  318 us (14%)
  matrix products  172 us (8%)
  other arithmetic  93.1 us (4%)
    all_to_all x1, blocking collectives, per_device(): lax.all_to_all(grad_buffer.reshape(expert_count, 1, grad_buffer.shape[1],...  346 us
    all_to_all x1, blocking collectives, per_device(): lax.all_to_all(buffer.reshape(expert_count, 1, buffer.shape[1], feat_widt...  346 us
    all_to_all x1, blocking collectives, per_device(): lax.all_to_all(grad_summed.astype(jnp.bfloat16), 'expert', split_axis=1,...  180 us
    all_to_all x1, blocking collectives, per_device(): lax.all_to_all(summed.astype(jnp.bfloat16), 'expert', split_axis=1, conca...  180 us
    reduce_scatter x1, waiting for transfers between devices, per_device(): lax.psum_scatter(output_weight_grad, ('dp', 'expert'), scatter_dimension=...  142 us
    reduce_scatter x1, waiting for transfers between devices, per_device(): lax.psum_scatter(query_grad, ('dp', 'expert'), scatter_dimension=0, tiled...  141 us
    unnamed x16, waiting for transfers between devices  130 us
    unnamed x139, local copies, waits for them, and re-layouts  111 us
  transfers between devices with their start and end apart: 12, of which 9 were waited for; matrix products, arithmetic and copies ran while one was open for 12% of the time, Pallas kernels for 0%

commit v1 on v0

v1 whole, which is shorter than its diff:
```python
import functools

import jax
import jax.numpy as jnp
from jax import lax
from jax.experimental import pallas as pl
from jax.experimental.pallas import tpu as pltpu
from jax.sharding import PartitionSpec as P

HEAD_SIZE = 64
TOPK = 8
SEQUENCE_LENGTH = 512


EPSILON = 1e-06
RESIDUAL = 0.22
ATTN_SCALE = 0.015625
ROPE_BASE = 10000.0
NEGATIVE = -1e30


def rotary_tables(length):
    half_dim = HEAD_SIZE // 2
    frequency = ROPE_BASE ** (-jnp.arange(half_dim, dtype=jnp.float32) * 2.0 / HEAD_SIZE)
    angles = jnp.arange(length, dtype=jnp.float32)[:, None] * frequency[None, :]
    return (jnp.cos(angles)[:, None, :], jnp.sin(angles)[:, None, :])


def rotate(value_rows, cosine, sine_table):
    half_dim = value_rows.shape[-1] // 2
    first = value_rows[..., :half_dim]
    second = value_rows[..., half_dim:]
    return jnp.concatenate(
        [first * cosine - second * sine_table, second * cosine + first * sine_table], axis=-1
    )


def rotate_back(grads, cosine, sine_table):
    half_dim = grads.shape[-1] // 2
    first = grads[..., :half_dim]
    second = grads[..., half_dim:]
    return jnp.concatenate(
        [first * cosine + second * sine_table, second * cosine - first * sine_table], axis=-1
    )


def norm_forward(value_rows):
    inv_rms = lax.rsqrt(jnp.mean(value_rows * value_rows, axis=-1, keepdims=True) + EPSILON)
    return (value_rows * inv_rms, inv_rms)


def norm_backward(grad_normed, gain, normal_unit, inv_rms):
    grad_unit = grad_normed * gain
    grad_input = inv_rms * (
        grad_unit - normal_unit * jnp.mean(grad_unit * normal_unit, axis=-1, keepdims=True)
    )
    return (grad_input, jnp.sum(grad_normed * normal_unit, axis=0))


def block_scores(query_block, key_block, row_start):
    scores = (
        jnp.einsum("sqjgd,skjd->sjgqk", query_block, key_block, preferred_element_type=jnp.float32)
        * ATTN_SCALE
    )
    row_ids = row_start + jnp.arange(query_block.shape[1])[:, None]
    col_ids = jnp.arange(key_block.shape[1])[None, :]
    return jnp.where(row_ids >= col_ids, scores, NEGATIVE)


def contract(left, right, left_dim, right_dim):
    return lax.dot_general(
        left, right, (((left_dim,), (right_dim,)), ((), ())), preferred_element_type=jnp.float32
    )


def experts_body(
    rows_ref,
    cot_ref,
    hits_ref,
    router_ref,
    gateup_ref,
    down_ref,
    comb_ref,
    grad_ref,
    act_ref,
    hidden_ref,
    gates_ref,
    comb_sum,
    grad_sum,
    dot_sum,
):
    step = pl.program_id(0)
    steps = pl.num_programs(0)
    hidden_units = down_ref.shape[1]
    feat_width = rows_ref.shape[1]
    number = lax.axis_index("expert") * steps + step
    lane = lax.broadcasted_iota(jnp.int32, hits_ref.shape, 1)

    @pl.when(step == 0)
    def _():
        hits = hits_ref[...] > 0
        logits = jnp.dot(rows_ref[...], router_ref[...], preferred_element_type=jnp.float32)
        logits = jnp.where(hits, logits, NEGATIVE)
        raised = jnp.where(hits, jnp.exp(logits - jnp.max(logits, axis=1, keepdims=True)), 0.0)
        gates_ref[...] = raised / jnp.sum(raised, axis=1, keepdims=True)

    rows = rows_ref[...]
    gate_part = jnp.dot(rows, gateup_ref[0, 0], preferred_element_type=jnp.float32)
    up_part = jnp.dot(rows, gateup_ref[0, 1], preferred_element_type=jnp.float32)
    raw = contract(cot_ref[...], down_ref[0], 1, 1)
    here = lane == number
    weight = jnp.sum(jnp.where(here, gates_ref[...], 0.0), axis=1, keepdims=True)
    sigmoid_gate = jax.nn.sigmoid(gate_part)
    silu_gate = gate_part * sigmoid_gate
    activation = silu_gate * up_part
    dots = jnp.where(here, jnp.sum(activation * raw, axis=1, keepdims=True), 0.0)
    weighted = (activation * weight).astype(jnp.bfloat16)
    act_ref[...] = weighted
    grad_act = raw * (RESIDUAL * weight)
    grad_gatepart = (
        grad_act * up_part * (sigmoid_gate * (1.0 + gate_part * (1.0 - sigmoid_gate)))
    ).astype(jnp.bfloat16)
    grad_uppart = (grad_act * silu_gate).astype(jnp.bfloat16)
    hidden_ref[:, :hidden_units] = grad_gatepart
    hidden_ref[:, hidden_units:] = grad_uppart
    comb = jnp.dot(weighted, down_ref[0], preferred_element_type=jnp.float32)
    grad = contract(grad_gatepart, gateup_ref[0, 0], 1, 1) + contract(
        grad_uppart, gateup_ref[0, 1], 1, 1
    )

    @pl.when(step == 0)
    def _():
        comb_sum[...] = comb
        grad_sum[...] = grad
        dot_sum[...] = dots

    @pl.when(step > 0)
    def _():
        comb_sum[...] += comb
        grad_sum[...] += grad
        dot_sum[...] += dots

    @pl.when(step == steps - 1)
    def _():
        comb_ref[...] = comb_sum[...].astype(jnp.bfloat16)
        grad_ref[:, :feat_width] = grad_sum[...].astype(jnp.bfloat16)
        grad_ref[:, feat_width:] = split_two(dot_sum[...])


def split_two(values):
    lane = lax.broadcasted_iota(jnp.int32, values.shape, 1)
    high = values.astype(jnp.bfloat16)
    low = values - high.astype(jnp.float32)
    half_lanes = values.shape[1] // 2
    moved = jnp.concatenate([low[:, half_lanes:], low[:, :half_lanes]], axis=1)
    return jnp.where(lane < half_lanes, high.astype(jnp.float32), moved).astype(jnp.bfloat16)


def experts(rows, cot, hits, router, gateup, down):
    count, feat_width = rows.shape
    local = gateup.shape[0]
    units = down.shape[1]
    lanes = hits.shape[1]
    whole = lambda step: (0, 0)
    return pl.pallas_call(
        experts_body,
        grid=(local,),
        in_specs=[
            pl.BlockSpec((count, feat_width), whole),
            pl.BlockSpec((count, feat_width), whole),
            pl.BlockSpec((count, lanes), whole),
            pl.BlockSpec((feat_width, lanes), whole),
            pl.BlockSpec((1, 2, feat_width, units), lambda step: (step, 0, 0, 0)),
            pl.BlockSpec((1, units, feat_width), lambda step: (step, 0, 0)),
        ],
        out_specs=[
            pl.BlockSpec((count, feat_width), whole),
            pl.BlockSpec((count, feat_width + lanes), whole),
            pl.BlockSpec((count, units), lambda step: (0, step)),
            pl.BlockSpec((count, 2 * units), lambda step: (0, step)),
            pl.BlockSpec((count, lanes), whole),
        ],
        out_shape=[
            jax.ShapeDtypeStruct((count, feat_width), jnp.bfloat16),
            jax.ShapeDtypeStruct((count, feat_width + lanes), jnp.bfloat16),
            jax.ShapeDtypeStruct((count, local * units), jnp.bfloat16),
            jax.ShapeDtypeStruct((count, local * 2 * units), jnp.bfloat16),
            jax.ShapeDtypeStruct((count, lanes), jnp.float32),
        ],
        scratch_shapes=[
            pltpu.VMEM((count, feat_width), jnp.float32),
            pltpu.VMEM((count, feat_width), jnp.float32),
            pltpu.VMEM((count, lanes), jnp.float32),
        ],
        compiler_params=pltpu.CompilerParams(vmem_limit_bytes=56 * 2**20),
        cost_estimate=pl.CostEstimate(
            flops=2 * count * feat_width * units * 6 * local,
            bytes_accessed=2 * (gateup.size + down.size) + 10 * count * feat_width,
            transcendentals=count * units * local,
        ),
    )(rows, cot, hits, router, gateup, down)


def weights_body(blocks, chunks, *refs):
    rows_refs, cot_refs = refs[:blocks], refs[blocks : 2 * blocks]
    act_refs, hidden_refs = refs[2 * blocks : 3 * blocks], refs[3 * blocks : 4 * blocks]
    gateup_ref, down_ref = refs[4 * blocks :]
    units = down_ref.shape[2]
    width = down_ref.shape[3]
    for part in range(2):
        total = sum(
            contract(rows_refs[b][...], hidden_refs[b][:, part * units : (part + 1) * units], 0, 0)
            for b in range(blocks)
        ).astype(jnp.bfloat16)
        for chunk in range(chunks):
            gateup_ref[chunk, 0, part] = total[chunk * width : (chunk + 1) * width]
    total = RESIDUAL * sum(
        contract(act_refs[b][...], cot_refs[b][...], 0, 0) for b in range(blocks)
    )
    total = total.astype(jnp.bfloat16)
    for chunk in range(chunks):
        down_ref[chunk, 0] = total[:, chunk * width : (chunk + 1) * width]


def expert_weights(rows, cots, acts, hiddens, chunks, local):
    blocks = len(rows)
    count, feat_width = rows[0].shape
    units = acts[0].shape[1] // local
    width = feat_width // chunks
    whole = lambda step: (0, 0)
    part = lambda step: (0, step)
    return pl.pallas_call(
        functools.partial(weights_body, blocks, chunks),
        grid=(local,),
        in_specs=[pl.BlockSpec((count, feat_width), whole)] * (2 * blocks)
        + [pl.BlockSpec((count, units), part)] * blocks
        + [pl.BlockSpec((count, 2 * units), part)] * blocks,
        out_specs=[
            pl.BlockSpec((chunks, 1, 2, width, units), lambda step: (0, step, 0, 0, 0)),
            pl.BlockSpec((chunks, 1, units, width), lambda step: (0, step, 0, 0)),
        ],
        out_shape=[
            jax.ShapeDtypeStruct((chunks, local, 2, width, units), jnp.bfloat16),
            jax.ShapeDtypeStruct((chunks, local, units, width), jnp.bfloat16),
        ],
        compiler_params=pltpu.CompilerParams(vmem_limit_bytes=56 * 2**20),
        cost_estimate=pl.CostEstimate(
            flops=2 * blocks * count * feat_width * units * 3 * local,
            bytes_accessed=4 * blocks * count * feat_width * 2 + 6 * local * units * feat_width,
            transcendentals=0,
        ),
    )(*rows, *cots, *acts, *hiddens)


def swap_cores(values):
    return lax.ppermute(values, "tensor", [(0, 1), (1, 0)])


def send_along(values, shift):
    count = lax.axis_size("expert")
    return lax.ppermute(values, "expert", [(i, (i + shift) % count) for i in range(count)])


def halving(values, steps, last):
    names = list(last)
    for axis, bit in steps:
        at = names.index((axis, bit))
        mine = (lax.axis_index(axis) >> bit) & 1
        keep = lax.dynamic_index_in_dim(values, mine, at, keepdims=False)
        send = lax.dynamic_index_in_dim(values, 1 - mine, at, keepdims=False)
        count = lax.axis_size(axis)
        got = lax.ppermute(send, axis, [(i, i ^ (1 << bit)) for i in range(count)])
        names.pop(at)
        values = keep.astype(jnp.float32) + got.astype(jnp.float32)
        if names:
            values = values.astype(send.dtype)
    return values


def bits_of(axis):
    return [(axis, bit) for bit in reversed(range(lax.axis_size(axis).bit_length() - 1))]


def per_device(
    tokens,
    out_grad,
    attn_gain,
    query_weight,
    key_value_weight,
    output_weight,
    expert_gain,
    router_weight,
    gateup_weight,
    down_weight,
    routes,
):
    tok_count, feat_width = tokens.shape
    expert_count = router_weight.shape[1]
    owners = lax.axis_size("expert")
    chunks = lax.axis_size("dp")
    core = lax.axis_index("tensor")
    local_experts = gateup_weight.shape[0]
    kv_heads = key_value_weight.shape[2] // HEAD_SIZE
    query_heads = query_weight.shape[1] // HEAD_SIZE
    groups = query_heads // kv_heads
    sequence_count = tok_count // SEQUENCE_LENGTH
    half = tok_count // 2
    lanes = 128
    dp_bits, owner_bits = bits_of("dp"), bits_of("expert")

    def halves(values):
        return (
            lax.dynamic_slice_in_dim(values, core * half, half, 0),
            lax.dynamic_slice_in_dim(values, (1 - core) * half, half, 0),
        )

    def in_order(mine, other):
        return jnp.where(
            core == 0,
            jnp.concatenate([mine, other], axis=0),
            jnp.concatenate([other, mine], axis=0),
        )

    def both_cores(mine):
        return jnp.concatenate([mine, swap_cores(mine)], axis=0)

    cot_mine, cot_other = halves(out_grad)
    cots = [jnp.concatenate([cot_mine, cot_other], axis=0)]
    hit_table = jnp.any(
        routes[:, :, None] == jnp.arange(lanes, dtype=jnp.int32)[None, None, :], axis=1
    ).astype(jnp.bfloat16)
    hits_mine, hits_other = halves(hit_table)
    hits = [jnp.concatenate([hits_mine, hits_other], axis=0)]
    for slot in range(1, owners):
        cots.append(both_cores(send_along(cot_mine, -slot)))
        hits.append(both_cores(send_along(hits_mine, -slot)))
    router_wide = jnp.pad(router_weight, ((0, 0), (0, lanes - expert_count)))

    cosine, sine_table = rotary_tables(SEQUENCE_LENGTH)
    inputs = tokens.astype(jnp.float32)
    unit_first, rms_first = norm_forward(inputs)
    normed = (unit_first * attn_gain).astype(jnp.bfloat16)
    queries = jnp.dot(normed, query_weight, preferred_element_type=jnp.float32)
    key_value = jnp.einsum(
        "td,cde->cte", normed, key_value_weight, preferred_element_type=jnp.float32
    )
    query_rot = (
        rotate(
            queries.reshape(sequence_count, SEQUENCE_LENGTH, query_heads, HEAD_SIZE),
            cosine,
            sine_table,
        )
        .astype(jnp.bfloat16)
        .reshape(sequence_count, SEQUENCE_LENGTH, kv_heads, groups, HEAD_SIZE)
    )
    keys_rot = rotate(
        key_value[0].reshape(sequence_count, SEQUENCE_LENGTH, kv_heads, HEAD_SIZE),
        cosine,
        sine_table,
    ).astype(jnp.bfloat16)
    value_rows = (
        key_value[1]
        .astype(jnp.bfloat16)
        .reshape(sequence_count, SEQUENCE_LENGTH, kv_heads, HEAD_SIZE)
    )
    scores = block_scores(query_rot, keys_rot, 0)
    row_max = jnp.max(scores, axis=-1, keepdims=True)
    exp_scores = jnp.exp(scores - row_max)
    row_sum = jnp.sum(exp_scores, axis=-1, keepdims=True)
    prob_block = (exp_scores / row_sum).astype(jnp.bfloat16)
    outputs = jnp.einsum(
        "sjgqk,skjd->sqjgd", prob_block, value_rows, preferred_element_type=jnp.float32
    )
    heads_out = outputs.astype(jnp.bfloat16).reshape(tok_count, query_heads * HEAD_SIZE)
    partial_value = jnp.dot(heads_out, output_weight, preferred_element_type=jnp.float32)

    part_mine, part_other = halves(partial_value)
    inputs_mine = halves(inputs)[0]
    middle = inputs_mine + RESIDUAL * (part_mine + swap_cores(part_other))
    unit_second, rms_second = norm_forward(middle)
    expert_in = (unit_second * expert_gain).astype(jnp.bfloat16)
    rows = [both_cores(expert_in)]
    for slot in range(1, owners):
        rows.append(both_cores(send_along(expert_in, -slot)))

    comb_total = jnp.zeros((half, feat_width), jnp.float32)
    grad_total = jnp.zeros((half, feat_width), jnp.float32)
    dots_total = jnp.zeros((half, lanes), jnp.float32)
    acts, hiddens = [None] * owners, [None] * owners
    gates = None
    for slot in range(owners):
        comb, grad, acts[slot], hiddens[slot], slot_gates = experts(
            rows[slot], cots[slot], hits[slot], router_wide, gateup_weight, down_weight
        )
        if slot == 0:
            gates = slot_gates[:half]
        comb = comb[:half].astype(jnp.float32) + swap_cores(comb[half:]).astype(jnp.float32)
        grad_other = swap_cores(grad[half:])
        grad_sum = grad[:half, :feat_width].astype(jnp.float32) + grad_other[
            :, :feat_width
        ].astype(jnp.float32)
        dots = grad[:half, feat_width:].astype(jnp.float32) + grad_other[:, feat_width:].astype(
            jnp.float32
        )
        if slot > 0:
            comb = send_along(comb.astype(jnp.bfloat16), slot).astype(jnp.float32)
            dots_whole = dots[:, : lanes // 2] + dots[:, lanes // 2 :]
            dots_whole = jnp.pad(dots_whole, ((0, 0), (0, lanes // 2)))
            back = send_along(
                jnp.concatenate([grad_sum.astype(jnp.bfloat16), split_two(dots_whole)], axis=1),
                slot,
            )
            grad_sum = back[:, :feat_width].astype(jnp.float32)
            dots = back[:, feat_width:].astype(jnp.float32)
        comb_total = comb_total + comb
        grad_total = grad_total + grad_sum
        dots_total = dots_total + dots

    mixed = (middle + RESIDUAL * comb_total).astype(jnp.bfloat16)
    output = in_order(mixed, swap_cores(mixed))

    gateup_grad, down_grad = expert_weights(rows, cots, acts, hiddens, chunks, local_experts)
    dp_shape = (2,) * len(dp_bits)
    parts = []
    for part in range(2):
        order = dp_bits if part == 0 else dp_bits[::-1]
        parts.append(
            (
                halving(
                    gateup_grad[:, :, part].reshape(dp_shape + (local_experts, feat_width // chunks, -1)),
                    order,
                    dp_bits,
                ),
                halving(
                    jnp.split(down_grad, 2, axis=2)[part].reshape(
                        dp_shape + (local_experts, -1, feat_width // chunks)
                    ),
                    order,
                    dp_bits,
                ),
            )
        )
    gateup_total = jnp.stack([parts[0][0], parts[1][0]], axis=1)
    down_total = jnp.concatenate([parts[0][1], parts[1][1]], axis=1)

    dots_whole = dots_total[:, : lanes // 2] + dots_total[:, lanes // 2 :]
    gates = gates[:, : lanes // 2]
    grad_gate = RESIDUAL * dots_whole
    grad_logits = gates * (grad_gate - jnp.sum(gates * grad_gate, axis=-1, keepdims=True))
    grad_logits = grad_logits[:, :expert_count].astype(jnp.bfloat16)
    grad_expert_in = grad_total + jnp.einsum(
        "te,de->td", grad_logits, router_weight, preferred_element_type=jnp.float32
    )
    router_grad = jnp.einsum(
        "te,td->ed", grad_logits, expert_in, preferred_element_type=jnp.float32
    )
    grad_middle_norm, expert_gain_grad = norm_backward(
        grad_expert_in, expert_gain, unit_second, rms_second
    )
    grad_middle = cot_mine.astype(jnp.float32) + grad_middle_norm
    grad_attn_mine = (RESIDUAL * grad_middle).astype(jnp.bfloat16)
    grad_attn = in_order(grad_attn_mine, swap_cores(grad_attn_mine))
    output_weight_grad = jnp.einsum(
        "td,te->de", grad_attn, heads_out, preferred_element_type=jnp.float32
    ).astype(jnp.bfloat16)
    grad_heads = (
        jnp.einsum("td,ed->te", grad_attn, output_weight, preferred_element_type=jnp.float32)
        .astype(jnp.bfloat16)
        .reshape(sequence_count, SEQUENCE_LENGTH, kv_heads, groups, HEAD_SIZE)
    )
    prob_block = exp_scores / row_sum
    grad_probs = jnp.einsum(
        "sqjgd,skjd->sjgqk", grad_heads, value_rows, preferred_element_type=jnp.float32
    )
    grad_values = jnp.einsum(
        "sjgqk,sqjgd->skjd",
        prob_block.astype(jnp.bfloat16),
        grad_heads,
        preferred_element_type=jnp.float32,
    )
    grad_scores = (
        prob_block * (grad_probs - jnp.sum(prob_block * grad_probs, axis=-1, keepdims=True))
    ).astype(jnp.bfloat16)
    grad_queries = (
        jnp.einsum("sjgqk,skjd->sqjgd", grad_scores, keys_rot, preferred_element_type=jnp.float32)
        * ATTN_SCALE
    )
    grad_keys = (
        jnp.einsum("sjgqk,sqjgd->skjd", grad_scores, query_rot, preferred_element_type=jnp.float32)
        * ATTN_SCALE
    )
    grad_query = (
        rotate_back(
            grad_queries.reshape(sequence_count, SEQUENCE_LENGTH, query_heads, HEAD_SIZE),
            cosine,
            sine_table,
        )
        .astype(jnp.bfloat16)
        .reshape(tok_count, query_heads * HEAD_SIZE)
    )
    grad_key = (
        rotate_back(grad_keys, cosine, sine_table)
        .astype(jnp.bfloat16)
        .reshape(tok_count, kv_heads * HEAD_SIZE)
    )
    grad_value = grad_values.astype(jnp.bfloat16).reshape(tok_count, kv_heads * HEAD_SIZE)
    grad_all = jnp.concatenate([grad_query, grad_key, grad_value], axis=1)
    weight_all = jnp.concatenate([query_weight, key_value_weight[0], key_value_weight[1]], axis=1)
    first_grad = jnp.einsum(
        "td,te->de", normed, grad_all, preferred_element_type=jnp.float32
    ).astype(jnp.bfloat16)
    grad_normed = jnp.einsum(
        "te,de->td", grad_all, weight_all, preferred_element_type=jnp.float32
    )
    normed_mine, normed_other = halves(grad_normed)
    grad_normed = normed_mine + swap_cores(normed_other.astype(jnp.bfloat16)).astype(jnp.float32)
    unit_mine, rms_mine = halves(unit_first)[0], halves(rms_first)[0]
    grad_first, attn_gain_grad = norm_backward(grad_normed, attn_gain, unit_mine, rms_mine)
    grad_tokens = grad_middle + grad_first
    tokens_grad = in_order(grad_tokens, swap_cores(grad_tokens))

    all_bits = dp_bits + owner_bits
    all_shape = (2,) * len(all_bits)
    pieces = chunks * owners

    def reduce_whole(values):
        columns = values.shape[1]
        out = []
        for part in range(2):
            order = (dp_bits if part == 0 else dp_bits[::-1]) + owner_bits[::-1]
            out.append(
                halving(
                    jnp.split(values, 2, axis=1)[part].reshape(
                        all_shape + (feat_width // pieces, columns // 2)
                    ),
                    order,
                    all_bits,
                )
            )
        return jnp.concatenate(out, axis=1)

    def reduce_small(values):
        values = values + swap_cores(values)
        values = values.reshape(values.shape[0], pieces, -1).transpose(1, 0, 2)
        return halving(values.reshape(all_shape + values.shape[1:]), all_bits[::-1], all_bits)

    output_total = reduce_whole(output_weight_grad).T
    first_total = reduce_whole(first_grad)
    small = reduce_small(jnp.concatenate([router_grad, expert_gain_grad[None]], axis=0))
    attn_gain_total = reduce_small(attn_gain_grad[None])[0]
    query_width = query_weight.shape[1]
    key_width = key_value_weight.shape[2]
    keyvalue_total = jnp.stack(
        [
            first_total[:, query_width : query_width + key_width],
            first_total[:, query_width + key_width :],
        ],
        axis=0,
    )
    return (
        output,
        tokens_grad,
        attn_gain_total,
        first_total[:, :query_width],
        keyvalue_total,
        output_total,
        small[expert_count],
        small[:expert_count].T,
        gateup_total,
        down_total,
    )


def solution(mesh):
    placed = (
        P(("dp", "expert"), None),
        P(("dp", "expert"), None),
        P(),
        P(None, "tensor"),
        P(None, None, "tensor"),
        P("tensor", None),
        P(),
        P(),
        P("expert", None, None, "tensor"),
        P("expert", "tensor", None),
        P(("dp", "expert"), None),
    )
    return jax.shard_map(
        per_device,
        mesh=mesh,
        in_specs=placed,
        out_specs=(
            P(("dp", "expert"), None),
            P(("dp", "expert"), None),
            P(("dp", "expert")),
            P(("dp", "expert"), "tensor"),
            P(None, ("dp", "expert"), "tensor"),
            P("tensor", ("dp", "expert")),
            P(("dp", "expert")),
            P(("dp", "expert"), None),
            P("expert", None, "dp", "tensor"),
            P("expert", "tensor", "dp"),
        ),
        check_vma=False,
    )
```

time: 2270 us -> 685 us (0.30)
  blocking collectives: 1130 us -> 0 us
  waiting for transfers between devices: 528 us -> 200 us
  local copies, waits for them, and re-layouts: 318 us -> 69.1 us
  starting transfers between devices: 1.79 us -> 163 us
  matrix products: 172 us -> 43.6 us
  Pallas kernels: 0 us -> 125 us
    all_to_all x4 -> x0, blocking collectives: 1050 us -> none  [the longest x1 346 us: per_device(): lax.all_to_all(grad_buffer.reshape(expert_count, 1, grad_buffer.shape[1],...]
    reduce_scatter x4 -> x0, waiting for transfers between devices: 367 us -> none  [the longest x1 142 us: per_device(): lax.psum_scatter(output_weight_grad, ('dp', 'expert'), scatter_dimension=...]
    ppermute x0 -> x72, waiting for transfers between devices: none -> 200 us  [the longest x32 121 us: halving(): got = lax.ppermute(send, axis, [(i, i ^ 1 << bit) for i in range(count)])]
    ppermute x0 -> x72, starting transfers between devices: none -> 163 us  [the longest x15 108 us: send_along(): lax.ppermute(values, 'expert', [(i, (i + shift) % count) for i in range(c...]
    gather x4 -> x0, local copies, waits for them, and re-layouts: 136 us -> none  [the longest x1 37.5 us: per_device(): jnp.concatenate([grad_pairs, jnp.zeros((1, feat_width), jnp.bfloat16)], a...]
    unnamed x16 -> x0, waiting for transfers between devices: 130 us -> none
    pallas_call x0 -> x5, Pallas kernels: none -> 125 us  [the longest x4 91.6 us: experts(): pl.pallas_call(experts_body, grid=(local,), in_specs=[pl.BlockSpec((count...]
    dot_general x13 -> x4, matrix products: 126 us -> 6.36 us  [the longest x1 2.45 us: per_device(): jnp.einsum('td,te->de', normed, grad_all, preferred_element_type=jnp.floa...]
  transfers between devices with their start and end apart: 12 -> 72, of which waited for: 9 -> 30; matrix products, arithmetic and copies ran while one was open for 12% -> 25% of each run, Pallas kernels for 0% -> 19%
where the time goes in v1:
time: 685 us; the launch traced here: 674 us
  waiting for transfers between devices  200 us (29%)
  starting transfers between devices  163 us (24%)
  Pallas kernels  125 us (18%)
  other arithmetic  70.5 us (10%)
  local copies, waits for them, and re-layouts  69.1 us (10%)
  matrix products  43.6 us (6%)
    ppermute x32, waiting for transfers between devices, halving(): got = lax.ppermute(send, axis, [(i, i ^ 1 << bit) for i in range(count)])  121 us
    ppermute x15, starting transfers between devices, send_along(): lax.ppermute(values, 'expert', [(i, (i + shift) % count) for i in range(c...  108 us
    pallas_call x4, Pallas kernels, experts(): pl.pallas_call(experts_body, grid=(local,), in_specs=[pl.BlockSpec((count...  91.6 us
    ppermute x15, waiting for transfers between devices, send_along(): lax.ppermute(values, 'expert', [(i, (i + shift) % count) for i in range(c...  75.4 us
    ppermute x32, starting transfers between devices, halving(): got = lax.ppermute(send, axis, [(i, i ^ 1 << bit) for i in range(count)])  50.7 us
    pallas_call x1, Pallas kernels, expert_weights(): pl.pallas_call(functools.partial(weights_body, blocks, chunks), grid=(loc...  33.7 us
    unnamed x188, local copies, waits for them, and re-layouts  23 us
  transfers between devices with their start and end apart: 72, of which 30 were waited for; matrix products, arithmetic and copies ran while one was open for 25% of the time, Pallas kernels for 19%

profile of v1, /device:TPU:0, one launch (start us, length us, event | category | flops | bytes accessed | tf_op | source)
XLA Modules:
  0.0 674.0 jit_solution(4172109681605313870)
XLA Ops:
  28.3 4.5 fusion.29
  41.2 3.7 collective-permute-done.23
  52.7 11.1 %collective-permute-done.15 = bf16[256,128]{1,0:T(8,128)(2,1)} collective-permute-done((bf16[256,128]{1,0:T(8,128)(2,1)S(1)}, bf16[256,128]{1,0:T(8,128)(2,1)}, u32[]{:S(2)}, u32[]{:S(2)}) %collective-permute-start.15) | collective-permute-done | bytes 65568 | tf_op jit(solution)/shard_map/ppermute | solution.py:261
  63.8 26.2 %collective-permute-start.7 = (bf16[256,128]{1,0:T(8,128)(2,1)S(1)}, bf16[256,128]{1,0:T(8,128)(2,1)S(1)}, u32[]{:S(2)}, u32[]{:S(2)}) collective-permute-start(bf16[256,128]{1,0:T(8,128)(2,1)S(1)} %get-tuple-element.93), channel_id=1, source_target_pairs={{0,6},{2,0},{4,2},{6,4},{1,7},{3,1},{5,3},{7,5},{8,14},{10,8},{12,... | collective-permute-start | bytes 196616 | tf_op jit(solution)/shard_map/ppermute | solution.py:261
  90.6 5.6 collective-permute-done.7
  115.6 14.4 %collective-permute-done.19 = bf16[256,1536]{1,0:T(8,128)(2,1)} collective-permute-done((bf16[256,1536]{1,0:T(8,128)(2,1)S(1)}, bf16[256,1536]{1,0:T(8,128)(2,1)}, u32[]{:S(2)}, u32[]{:S(2)}) %collective-permute-start.19) | collective-permute-done | bytes 786464 | tf_op jit(solution)/shard_map/ppermute | solution.py:261
  131.3 22.8 %shard_map.186 = (bf16[512,1536]{1,0:T(8,128)(2,1)}, bf16[512,1664]{1,0:T(8,128)(2,1)}, bf16[512,1280]{1,0:T(8,128)(2,1)}, bf16[512,2560]{1,0:T(8,128)(2,1)}, f32[512,128]{1,0:T(8,128)}) custom-call(bf16[512,1536]{1,0:T(8,128)(2,1)} %pad_maximum_fusion.2.rows_ref.refs_0_, bf16[512,1536]{1,0:T(8,128)(2,1)} %pad_maximum_fusion.3.cot_ref.refs_4_, ...), custom_call_target="tpu_custom_call" | custom-call | flops 12079595520 | bytes 19660800 | tf_op jit(solution)/shard_map/pallas_call | solution.py:165
  157.9 5.2 collective-permute-done.11
  171.9 22.8 %shard_map.189 = (bf16[512,1536]{1,0:T(8,128)(2,1)}, bf16[512,1664]{1,0:T(8,128)(2,1)}, bf16[512,1280]{1,0:T(8,128)(2,1)}, bf16[512,2560]{1,0:T(8,128)(2,1)}, f32[512,128]{1,0:T(8,128)}) custom-call(bf16[512,1536]{1,0:T(8,128)(2,1)} %constant_dynamic-update-slice_fusion.8.rows_ref.refs_3_, bf16[512,1536]{1,0:T(8,128)(2,1)} %copy-done.62, ...), custom_call_target="tpu_custom_call" | custom-call | flops 12079595520 | bytes 19660800 | tf_op jit(solution)/shard_map/pallas_call | solution.py:165
  195.7 23.1 %shard_map.188 = (bf16[512,1536]{1,0:T(8,128)(2,1)}, bf16[512,1664]{1,0:T(8,128)(2,1)}, bf16[512,1280]{1,0:T(8,128)(2,1)}, bf16[512,2560]{1,0:T(8,128)(2,1)}, f32[512,128]{1,0:T(8,128)}) custom-call(bf16[512,1536]{1,0:T(8,128)(2,1)} %constant_dynamic-update-slice_fusion.4.rows_ref.refs_2_, bf16[512,1536]{1,0:T(8,128)(2,1)} %copy-done.61, ...), custom_call_target="tpu_custom_call" | custom-call | flops 12079595520 | bytes 19660800 | tf_op jit(solution)/shard_map/pallas_call | solution.py:165
  219.7 22.8 %shard_map.187 = (bf16[512,1536]{1,0:T(8,128)(2,1)}, bf16[512,1664]{1,0:T(8,128)(2,1)}, bf16[512,1280]{1,0:T(8,128)(2,1)}, bf16[512,2560]{1,0:T(8,128)(2,1)}, f32[512,128]{1,0:T(8,128)}) custom-call(bf16[512,1536]{1,0:T(8,128)(2,1)} %constant_dynamic-update-slice_fusion.rows_ref.refs_1_, bf16[512,1536]{1,0:T(8,128)(2,1)} %copy-done.63, ...), custom_call_target="tpu_custom_call" | custom-call | flops 12079595520 | bytes 19660800 | tf_op jit(solution)/shard_map/pallas_call | solution.py:165
  242.6 33.7 %shard_map.190 = (bf16[4,5,2,384,256]{4,3,2,1,0:T(8,128)(2,1)}, bf16[4,5,256,384]{3,2,1,0:T(8,128)(2,1)}) custom-call(bf16[512,1536]{1,0:T(8,128)(2,1)} %pad_maximum_fusion.2.rows_ref.refs_0_, bf16[512,1536]{1,0:T(8,128)(2,1)} %constant_dynamic-update-slice_fusion.rows_ref.refs_1_, bf16[512,1536]{1,0:T(8,128)(2,1)} %constant_dynamic-update-slice_fusion.4.rows_ref.refs_2_, ...), custom_call_target="tpu_custom_call" | custom-call | flops 24159191040 | bytes 36962304 | tf_op jit(solution)/shard_map/pallas_call | solution.py:232
  303.0 28.0 %collective-permute-start.30 = (bf16[256,1664]{1,0:T(8,128)(2,1)S(1)}, bf16[256,1664]{1,0:T(8,128)(2,1)S(1)}, u32[]{:S(2)}, u32[]{:S(2)}) collective-permute-start(bf16[256,1664]{1,0:T(8,128)(2,1)S(1)} %pad_maximum_fusion.5), channel_id=1, source_target_pairs={{0,2},{2,4},{4,6},{6,0},{1,3},{3,5},{5,7},{7,1},{8,10},{10,12},{12... | collective-permute-start | bytes 2555912 | tf_op jit(solution)/shard_map/ppermute | solution.py:261
  342.4 7.9 %collective-permute-done.30 = bf16[256,1664]{1,0:T(8,128)(2,1)S(1)} collective-permute-done((bf16[256,1664]{1,0:T(8,128)(2,1)S(1)}, bf16[256,1664]{1,0:T(8,128)(2,1)S(1)}, u32[]{:S(2)}, u32[]{:S(2)}) %collective-permute-start.30) | collective-permute-done | bytes 852000 | tf_op jit(solution)/shard_map/ppermute | solution.py:261
  350.8 27.6 %collective-permute-done.32 = bf16[256,1664]{1,0:T(8,128)(2,1)S(1)} collective-permute-done((bf16[256,1664]{1,0:T(8,128)(2,1)S(1)}, bf16[256,1664]{1,0:T(8,128)(2,1)S(1)}, u32[]{:S(2)}, u32[]{:S(2)}) %collective-permute-start.32) | collective-permute-done | bytes 852000 | tf_op jit(solution)/shard_map/ppermute | solution.py:261
  378.4 31.6 %collective-permute-start.26 = (bf16[256,1536]{1,0:T(8,128)(2,1)}, bf16[256,1536]{1,0:T(8,128)(2,1)}, u32[]{:S(2)}, u32[]{:S(2)}) collective-permute-start(bf16[256,1536]{1,0:T(8,128)(2,1)} %add_convert_fusion.4), channel_id=1, source_target_pairs={{0,6},{2,0},{4,2},{6,4},{1,7},{3,1},{5,3},{7,5},{8,14},{10,8},{12,... | collective-permute-start | bytes 2359304 | tf_op jit(solution)/shard_map/ppermute | solution.py:261
  411.8 3.8 multiply_reduce_fusion.1
  415.8 6.3 collective-permute-done.69
  426.1 11.1 %collective-permute-done.71 = bf16[5,128,384]{2,1,0:T(8,128)(2,1)} collective-permute-done((bf16[5,128,384]{2,1,0:T(8,128)(2,1)}, bf16[5,128,384]{2,1,0:T(8,128)(2,1)}, u32[]{:S(2)}, u32[]{:S(2)}) %collective-permute-start.71) | collective-permute-done | bytes 491552 | tf_op jit(solution)/shard_map/ppermute | solution.py:272
  437.2 21.3 %collective-permute-start.60 = (f32[2,2,2,21,96]{4,2,1,0,3:T(2,128)S(1)}, f32[2,2,2,21,96]{4,2,1,0,3:T(2,128)S(1)}, u32[]{:S(2)}, u32[]{:S(2)}) collective-permute-start(f32[2,2,2,21,96]{4,2,1,0,3:T(2,128)S(1)} %bitcast.367), channel_id=1, source_target_pairs={{0,2},{2,0},{4,6},{6,4},{1,3},{3,1},{5,7},{7,5},{8,10},{10,8},{12,... | collective-permute-start | bytes 193544 | tf_op jit(solution)/shard_map/ppermute | solution.py:272
  461.1 4.2 collective-permute-start.61
  490.5 11.2 %fusion = (f32[4,3,512]{2,1,0:T(4,128)S(1)}, f32[4,512,512,3]{2,1,3,0:T(8,128)}) fusion(f32[4,3,512]{2,1,0:T(4,128)S(1)} %copy-done.67, f32[4,3,512]{2,1,0:T(4,128)S(1)} %copy-done.65, f32[4,512,512,3]{2,1,3,0:T(8,128)} %copy-done.1, pred[512,512]{0,1:T(8,128)(4,1)S(1)} %iota_compare_fusion.1, bf16[512,4,64,1]{0,2,3,1:T(8,128)(2,1)} %bitcast.364, ...), kind=kOutput, calls=%fused_computation.3 | convolution fusion | flops 421521408 | bytes 26550272 | tf_op jit(solution)/shard_map/sqjgd,skjd->sjgqk/dot_general | solution.py:472
  503.4 7.0 %fusion.6 = bf16[4,3,512,512]{2,3,1,0:T(8,128)(2,1)S(1)} fusion(f32[4,512,512,3]{2,1,3,0:T(8,128)} %get-tuple-element.114, f32[4,3,512]{2,1,0:T(4,128)S(1)} %get-tuple-element.113, f32[4,3,512]{2,1,0:T(4,128)S(1)} %copy-done.67, f32[4,3,512]{2,1,0:T(4,128)S(1)} %copy-done.65, f32[4,512,512,3]{2,1,3,0:T(8,128)S(1)} %bitcast.329, ...), kind=kLoop, calls=%fused_computation.11 | loop fusion | flops 22020096 | bytes 31793152 | tf_op jit(solution)/shard_map/reshape.38
  514.5 3.6 fusion.40
  546.2 5.8 collective-permute-done.55
  554.7 23.6 %collective-permute-done.39 = f32[2,2,2,1,96]{4,2,1,0,3:T(2,128)S(1)} collective-permute-done((f32[2,2,2,1,96]{4,2,1,0,3:T(2,128)S(1)}, f32[2,2,2,1,96]{4,2,1,0,3:T(2,128)S(1)}, u32[]{:S(2)}, u32[]{:S(2)}) %collective-permute-start.39) | collective-permute-done | bytes 3104 | tf_op jit(solution)/shard_map/ppermute | solution.py:272
  580.7 15.3 %collective-permute-done.40 = f32[2,2,1,96]{3,1,0,2:T(2,128)S(1)} collective-permute-done((f32[2,2,1,96]{3,1,0,2:T(2,128)S(1)}, f32[2,2,1,96]{3,1,0,2:T(2,128)S(1)}, u32[]{:S(2)}, u32[]{:S(2)}) %collective-permute-start.40) | collective-permute-done | bytes 1568 | tf_op jit(solution)/shard_map/ppermute | solution.py:272
  604.7 5.2 multiply_add_fusion
  609.9 19.2 %collective-permute-done.42 = f32[1,96]{1,0:T(1,128)S(1)} collective-permute-done((f32[1,96]{1,0:T(1,128)S(1)}, f32[1,96]{1,0:T(1,128)S(1)}, u32[]{:S(2)}, u32[]{:S(2)}) %collective-permute-start.42) | collective-permute-done | bytes 416 | tf_op jit(solution)/shard_map/ppermute | solution.py:272
  639.3 5.7 collective-permute-done.54
  645.1 5.3 collective-permute-done.58
  655.5 4.9 collective-permute-done.49
  (493 shorter events, 226.8 us)
Async XLA Ops:
  3.2 98.7 %collective-permute-start.21 = (bf16[256,1536]{1,0:T(8,128)(2,1)S(1)}, bf16[256,1536]{1,0:T(8,128)(2,1)}, u32[]{:S(2)}, u32[]{:S(2)}) collective-permute-start(bf16[256,1536]{1,0:T(8,128)(2,1)S(1)} %get-tuple-element.78), channel_id=1, source_target_pairs={{0,2},{2,4},{4,6},{6,0},{1,3},{3,5},{5,7},{7,1},{8,10},{10,12},{12... | collective-permute-start | bytes 2359304 | tf_op jit(solution)/shard_map/ppermute | solution.py:261
  6.2 95.8 %collective-permute-start.13 = (bf16[256,1536]{1,0:T(8,128)(2,1)S(1)}, bf16[256,1536]{1,0:T(8,128)(2,1)}, u32[]{:S(2)}, u32[]{:S(2)}) collective-permute-start(bf16[256,1536]{1,0:T(8,128)(2,1)S(1)} %get-tuple-element.78), channel_id=1, source_target_pairs={{0,4},{2,6},{4,0},{6,2},{1,5},{3,7},{5,1},{7,3},{8,12},{10,14},{12... | collective-permute-start | bytes 2359304 | tf_op jit(solution)/shard_map/ppermute | solution.py:261
  11.9 33.0 %collective-permute-start.23 = (bf16[256,128]{1,0:T(8,128)(2,1)S(1)}, bf16[256,128]{1,0:T(8,128)(2,1)}, u32[]{:S(2)}, u32[]{:S(2)}) collective-permute-start(bf16[256,128]{1,0:T(8,128)(2,1)S(1)} %get-tuple-element.93), channel_id=1, source_target_pairs={{0,2},{2,4},{4,6},{6,0},{1,3},{3,5},{5,7},{7,1},{8,10},{10,12},{12... | collective-permute-start | bytes 196616 | tf_op jit(solution)/shard_map/ppermute | solution.py:261
  12.0 51.8 %collective-permute-start.15 = (bf16[256,128]{1,0:T(8,128)(2,1)S(1)}, bf16[256,128]{1,0:T(8,128)(2,1)}, u32[]{:S(2)}, u32[]{:S(2)}) collective-permute-start(bf16[256,128]{1,0:T(8,128)(2,1)S(1)} %get-tuple-element.93), channel_id=1, source_target_pairs={{0,4},{2,6},{4,0},{6,2},{1,5},{3,7},{5,1},{7,3},{8,12},{10,14},{12... | collective-permute-start | bytes 196616 | tf_op jit(solution)/shard_map/ppermute | solution.py:261
  37.3 67.7 %collective-permute-start = (f32[256,1536]{1,0:T(8,128)}, f32[256,1536]{1,0:T(8,128)}, u32[]{:S(2)}, u32[]{:S(2)}) collective-permute-start(f32[256,1536]{1,0:T(8,128)} %constant_dynamic-slice_fusion.26), channel_id=1, source_target_pairs={{0,1},{1,0},{2,3},{3,2},{4,5},{5,4},{6,7},{7,6},{8,9},{9,8},{10,11... | collective-permute-start | bytes 4718600 | tf_op jit(solution)/shard_map/ppermute | solution.py:256
  44.9 57.4 %collective-permute-start.5 = (bf16[256,1536]{1,0:T(8,128)(2,1)S(1)}, bf16[256,1536]{1,0:T(8,128)(2,1)}, u32[]{:S(2)}, u32[]{:S(2)}) collective-permute-start(bf16[256,1536]{1,0:T(8,128)(2,1)S(1)} %get-tuple-element.78), channel_id=1, source_target_pairs={{0,6},{2,0},{4,2},{6,4},{1,7},{3,1},{5,3},{7,5},{8,14},{10,8},{12,... | collective-permute-start | bytes 2359304 | tf_op jit(solution)/shard_map/ppermute | solution.py:261
  63.8 32.4 %collective-permute-start.7 = (bf16[256,128]{1,0:T(8,128)(2,1)S(1)}, bf16[256,128]{1,0:T(8,128)(2,1)S(1)}, u32[]{:S(2)}, u32[]{:S(2)}) collective-permute-start(bf16[256,128]{1,0:T(8,128)(2,1)S(1)} %get-tuple-element.93), channel_id=1, source_target_pairs={{0,6},{2,0},{4,2},{6,4},{1,7},{3,1},{5,3},{7,5},{8,14},{10,8},{12,... | collective-permute-start | bytes 196616 | tf_op jit(solution)/shard_map/ppermute | solution.py:261
  111.2 51.9 %collective-permute-start.11 = (bf16[256,1536]{1,0:T(8,128)(2,1)S(1)}, bf16[256,1536]{1,0:T(8,128)(2,1)}, u32[]{:S(2)}, u32[]{:S(2)}) collective-permute-start(bf16[256,1536]{1,0:T(8,128)(2,1)S(1)} %multiply_convert_fusion.2), channel_id=1, source_target_pairs={{0,4},{2,6},{4,0},{6,2},{1,5},{3,7},{5,1},{7,3},{8,12},{10,14},{12... | collective-permute-start | bytes 2359304 | tf_op jit(solution)/shard_map/ppermute | solution.py:261
  112.8 50.2 %collective-permute-start.3 = (bf16[256,1536]{1,0:T(8,128)(2,1)S(1)}, bf16[256,1536]{1,0:T(8,128)(2,1)}, u32[]{:S(2)}, u32[]{:S(2)}) collective-permute-start(bf16[256,1536]{1,0:T(8,128)(2,1)S(1)} %multiply_convert_fusion.2), channel_id=1, source_target_pairs={{0,6},{2,0},{4,2},{6,4},{1,7},{3,1},{5,3},{7,5},{8,14},{10,8},{12,... | collective-permute-start | bytes 2359304 | tf_op jit(solution)/shard_map/ppermute | solution.py:261
  130.0 39.8 %collective-permute-start.20 = (bf16[256,1536]{1,0:T(8,128)(2,1)}, bf16[256,1536]{1,0:T(8,128)(2,1)}, u32[]{:S(2)}, u32[]{:S(2)}) collective-permute-start(bf16[256,1536]{1,0:T(8,128)(2,1)} %collective-permute-done.19), channel_id=1, source_target_pairs={{0,1},{1,0},{2,3},{3,2},{4,5},{5,4},{6,7},{7,6},{8,9},{9,8},{10,11... | collective-permute-start | bytes 2359304 | tf_op jit(solution)/shard_map/ppermute | solution.py:256
  156.4 185.5 %collective-permute-start.28 = (bf16[256,1664]{1,0:T(8,128)(2,1)}, bf16[256,1664]{1,0:T(8,128)(2,1)}, u32[]{:S(2)}, u32[]{:S(2)}) collective-permute-start(bf16[256,1664]{1,0:T(8,128)(2,1)} %slice.226), channel_id=1, source_target_pairs={{0,1},{1,0},{2,3},{3,2},{4,5},{5,4},{6,7},{7,6},{8,9},{9,8},{10,11... | collective-permute-start | bytes 2555912 | tf_op jit(solution)/shard_map/ppermute | solution.py:256
  163.1 31.7 %collective-permute-start.12 = (bf16[256,1536]{1,0:T(8,128)(2,1)}, bf16[256,1536]{1,0:T(8,128)(2,1)S(1)}, u32[]{:S(2)}, u32[]{:S(2)}) collective-permute-start(bf16[256,1536]{1,0:T(8,128)(2,1)} %collective-permute-done.11), channel_id=1, source_target_pairs={{0,1},{1,0},{2,3},{3,2},{4,5},{5,4},{6,7},{7,6},{8,9},{9,8},{10,11... | collective-permute-start | bytes 2359304 | tf_op jit(solution)/shard_map/ppermute | solution.py:256
  163.1 55.7 %collective-permute-start.4 = (bf16[256,1536]{1,0:T(8,128)(2,1)}, bf16[256,1536]{1,0:T(8,128)(2,1)S(1)}, u32[]{:S(2)}, u32[]{:S(2)}) collective-permute-start(bf16[256,1536]{1,0:T(8,128)(2,1)} %collective-permute-done.3), channel_id=1, source_target_pairs={{0,1},{1,0},{2,3},{3,2},{4,5},{5,4},{6,7},{7,6},{8,9},{9,8},{10,11... | collective-permute-start | bytes 2359304 | tf_op jit(solution)/shard_map/ppermute | solution.py:256
  280.2 53.6 %collective-permute-start.68 = (bf16[2,5,128,384]{3,2,1,0:T(8,128)(2,1)}, bf16[2,5,128,384]{3,2,1,0:T(8,128)(2,1)}, u32[]{:S(2)}, u32[]{:S(2)}) collective-permute-start(bf16[2,5,128,384]{3,2,1,0:T(8,128)(2,1)} %dynamic-slice_bitcast_fusion.3), channel_id=1, source_target_pairs={{0,16},{8,24},{16,0},{24,8},{1,17},{9,25},{17,1},{25,9},{2,18},{10... | collective-permute-start | bytes 2949128 | tf_op jit(solution)/shard_map/ppermute | solution.py:272
  282.8 56.6 %collective-permute-start.70 = (bf16[2,5,128,384]{3,2,1,0:T(8,128)(2,1)}, bf16[2,5,128,384]{3,2,1,0:T(8,128)(2,1)}, u32[]{:S(2)}, u32[]{:S(2)}) collective-permute-start(bf16[2,5,128,384]{3,2,1,0:T(8,128)(2,1)} %dynamic-slice_bitcast_fusion.2), channel_id=1, source_target_pairs={{0,8},{8,0},{16,24},{24,16},{1,9},{9,1},{17,25},{25,17},{2,10},{10... | collective-permute-start | bytes 2949128 | tf_op jit(solution)/shard_map/ppermute | solution.py:272
  300.3 31.2 %collective-permute-start.9 = (bf16[256,1536]{1,0:T(8,128)(2,1)}, bf16[256,1536]{1,0:T(8,128)(2,1)S(1)}, u32[]{:S(2)}, u32[]{:S(2)}) collective-permute-start(bf16[256,1536]{1,0:T(8,128)(2,1)} %slice.220), channel_id=1, source_target_pairs={{0,1},{1,0},{2,3},{3,2},{4,5},{5,4},{6,7},{7,6},{8,9},{9,8},{10,11... | collective-permute-start | bytes 2359304 | tf_op jit(solution)/shard_map/ppermute | solution.py:256
  303.0 47.3 %collective-permute-start.30 = (bf16[256,1664]{1,0:T(8,128)(2,1)S(1)}, bf16[256,1664]{1,0:T(8,128)(2,1)S(1)}, u32[]{:S(2)}, u32[]{:S(2)}) collective-permute-start(bf16[256,1664]{1,0:T(8,128)(2,1)S(1)} %pad_maximum_fusion.5), channel_id=1, source_target_pairs={{0,2},{2,4},{4,6},{6,0},{1,3},{3,5},{5,7},{7,1},{8,10},{10,12},{12... | collective-permute-start | bytes 2555912 | tf_op jit(solution)/shard_map/ppermute | solution.py:261
  331.5 46.9 %collective-permute-start.32 = (bf16[256,1664]{1,0:T(8,128)(2,1)S(1)}, bf16[256,1664]{1,0:T(8,128)(2,1)S(1)}, u32[]{:S(2)}, u32[]{:S(2)}) collective-permute-start(bf16[256,1664]{1,0:T(8,128)(2,1)S(1)} %pad_maximum_fusion.6), channel_id=1, source_target_pairs={{0,4},{2,6},{4,0},{6,2},{1,5},{3,7},{5,1},{7,3},{8,12},{10,14},{12... | collective-permute-start | bytes 2555912 | tf_op jit(solution)/shard_map/ppermute | solution.py:261
  333.8 76.2 %collective-permute-start.34 = (bf16[256,1664]{1,0:T(8,128)(2,1)S(1)}, bf16[256,1664]{1,0:T(8,128)(2,1)S(1)}, u32[]{:S(2)}, u32[]{:S(2)}) collective-permute-start(bf16[256,1664]{1,0:T(8,128)(2,1)S(1)} %pad_maximum_fusion.7), channel_id=1, source_target_pairs={{0,6},{2,0},{4,2},{6,4},{1,7},{3,1},{5,3},{7,5},{8,14},{10,8},{12,... | collective-permute-start | bytes 2555912 | tf_op jit(solution)/shard_map/ppermute | solution.py:261
  339.4 260.8 %collective-permute-start.2 = (bf16[256,1536]{1,0:T(8,128)(2,1)}, bf16[256,1536]{1,0:T(8,128)(2,1)}, u32[]{:S(2)}, u32[]{:S(2)}) collective-permute-start(bf16[256,1536]{1,0:T(8,128)(2,1)} %slice.218), channel_id=1, source_target_pairs={{0,1},{1,0},{2,3},{3,2},{4,5},{5,4},{6,7},{7,6},{8,9},{9,8},{10,11... | collective-permute-start | bytes 2359304 | tf_op jit(solution)/shard_map/ppermute | solution.py:256
  341.9 134.9 %collective-permute-start.64 = (bf16[2,5,384,256]{3,2,1,0:T(8,128)(2,1)}, bf16[2,5,384,256]{3,2,1,0:T(8,128)(2,1)}, u32[]{:S(2)}, u32[]{:S(2)}) collective-permute-start(bf16[2,5,384,256]{3,2,1,0:T(8,128)(2,1)} %dynamic-slice_bitcast_fusion.1), channel_id=1, source_target_pairs={{0,16},{8,24},{16,0},{24,8},{1,17},{9,25},{17,1},{25,9},{2,18},{10... | collective-permute-start | bytes 5898248 | tf_op jit(solution)/shard_map/ppermute | solution.py:272
  350.3 130.4 %collective-permute-start.66 = (bf16[2,5,384,256]{3,2,1,0:T(8,128)(2,1)}, bf16[2,5,384,256]{3,2,1,0:T(8,128)(2,1)}, u32[]{:S(2)}, u32[]{:S(2)}) collective-permute-start(bf16[2,5,384,256]{3,2,1,0:T(8,128)(2,1)} %dynamic-slice_bitcast_fusion), channel_id=1, source_target_pairs={{0,8},{8,0},{16,24},{24,16},{1,9},{9,1},{17,25},{25,17},{2,10},{10... | collective-permute-start | bytes 5898248 | tf_op jit(solution)/shard_map/ppermute | solution.py:272
  378.4 222.8 %collective-permute-start.26 = (bf16[256,1536]{1,0:T(8,128)(2,1)}, bf16[256,1536]{1,0:T(8,128)(2,1)}, u32[]{:S(2)}, u32[]{:S(2)}) collective-permute-start(bf16[256,1536]{1,0:T(8,128)(2,1)} %add_convert_fusion.4), channel_id=1, source_target_pairs={{0,6},{2,0},{4,2},{6,4},{1,7},{3,1},{5,3},{7,5},{8,14},{10,8},{12,... | collective-permute-start | bytes 2359304 | tf_op jit(solution)/shard_map/ppermute | solution.py:261
  480.1 53.8 %collective-permute-start.65 = (bf16[5,384,256]{2,1,0:T(8,128)(2,1)}, bf16[5,384,256]{2,1,0:T(8,128)(2,1)}, u32[]{:S(2)}, u32[]{:S(2)}) collective-permute-start(bf16[5,384,256]{2,1,0:T(8,128)(2,1)} %dynamic-slice_bitcast_fusion.5), channel_id=1, source_target_pairs={{0,8},{8,0},{16,24},{24,16},{1,9},{9,1},{17,25},{25,17},{2,10},{10... | collective-permute-start | bytes 2949128 | tf_op jit(solution)/shard_map/ppermute | solution.py:272
  484.4 52.2 %collective-permute-start.67 = (bf16[5,384,256]{2,1,0:T(8,128)(2,1)}, bf16[5,384,256]{2,1,0:T(8,128)(2,1)}, u32[]{:S(2)}, u32[]{:S(2)}) collective-permute-start(bf16[5,384,256]{2,1,0:T(8,128)(2,1)} %dynamic-slice_bitcast_fusion.4), channel_id=1, source_target_pairs={{0,16},{8,24},{16,0},{24,8},{1,17},{9,25},{17,1},{25,9},{2,18},{10... | collective-permute-start | bytes 2949128 | tf_op jit(solution)/shard_map/ppermute | solution.py:272
  541.9 60.7 %collective-permute-start.18 = (bf16[256,1536]{1,0:T(8,128)(2,1)}, bf16[256,1536]{1,0:T(8,128)(2,1)}, u32[]{:S(2)}, u32[]{:S(2)}) collective-permute-start(bf16[256,1536]{1,0:T(8,128)(2,1)} %add_convert_fusion.5), channel_id=1, source_target_pairs={{0,4},{2,6},{4,0},{6,2},{1,5},{3,7},{5,1},{7,3},{8,12},{10,14},{12... | collective-permute-start | bytes 2359304 | tf_op jit(solution)/shard_map/ppermute | solution.py:261
  545.3 58.5 %collective-permute-start.10 = (bf16[256,1536]{1,0:T(8,128)(2,1)}, bf16[256,1536]{1,0:T(8,128)(2,1)}, u32[]{:S(2)}, u32[]{:S(2)}) collective-permute-start(bf16[256,1536]{1,0:T(8,128)(2,1)} %add_convert_fusion.6), channel_id=1, source_target_pairs={{0,2},{2,4},{4,6},{6,0},{1,3},{3,5},{5,7},{7,1},{8,10},{10,12},{12... | collective-permute-start | bytes 2359304 | tf_op jit(solution)/shard_map/ppermute | solution.py:261
  599.6 30.9 %collective-permute-start.47 = (bf16[2,2,2,96,640]{4,3,1,2,0:T(8,128)(2,1)}, bf16[2,2,2,96,640]{4,3,1,2,0:T(8,128)(2,1)S(1)}, u32[]{:S(2)}, u32[]{:S(2)}) collective-permute-start(bf16[2,2,2,96,640]{4,3,1,2,0:T(8,128)(2,1)} %bitcast.352), channel_id=1, source_target_pairs={{0,8},{8,0},{16,24},{24,16},{1,9},{9,1},{17,25},{25,17},{2,10},{10... | collective-permute-start | bytes 2949128 | tf_op jit(solution)/shard_map/ppermute | solution.py:272
  600.2 32.7 %collective-permute-start.43 = (bf16[2,2,2,96,640]{4,3,1,2,0:T(8,128)(2,1)}, bf16[2,2,2,96,640]{4,3,1,2,0:T(8,128)(2,1)S(1)}, u32[]{:S(2)}, u32[]{:S(2)}) collective-permute-start(bf16[2,2,2,96,640]{4,3,1,2,0:T(8,128)(2,1)} %bitcast.351), channel_id=1, source_target_pairs={{0,16},{8,24},{16,0},{24,8},{1,17},{9,25},{17,1},{25,9},{2,18},{10... | collective-permute-start | bytes 2949128 | tf_op jit(solution)/shard_map/ppermute | solution.py:272
  601.1 28.5 %collective-permute-start.52 = (bf16[2,2,96,384]{3,2,0,1:T(8,128)(2,1)S(1)}, bf16[2,2,96,384]{3,2,0,1:T(8,128)(2,1)S(1)}, u32[]{:S(2)}, u32[]{:S(2)}) collective-permute-start(bf16[2,2,96,384]{3,2,0,1:T(8,128)(2,1)S(1)} %dynamic-slice_bitcast_fusion.11), channel_id=1, source_target_pairs={{0,8},{8,0},{16,24},{24,16},{1,9},{9,1},{17,25},{25,17},{2,10},{10... | collective-permute-start | bytes 884744 | tf_op jit(solution)/shard_map/ppermute | solution.py:272
  602.6 27.6 %collective-permute-start.56 = (bf16[2,2,96,384]{3,2,0,1:T(8,128)(2,1)S(1)}, bf16[2,2,96,384]{3,2,0,1:T(8,128)(2,1)S(1)}, u32[]{:S(2)}, u32[]{:S(2)}) collective-permute-start(bf16[2,2,96,384]{3,2,0,1:T(8,128)(2,1)S(1)} %dynamic-slice_bitcast_fusion.10), channel_id=1, source_target_pairs={{0,16},{8,24},{16,0},{24,8},{1,17},{9,25},{17,1},{25,9},{2,18},{10... | collective-permute-start | bytes 884744 | tf_op jit(solution)/shard_map/ppermute | solution.py:272
  629.1 42.5 %collective-permute-start.37 = (f32[256,1536]{1,0:T(8,128)S(1)}, f32[256,1536]{1,0:T(8,128)S(1)}, u32[]{:S(2)}, u32[]{:S(2)}) collective-permute-start(f32[256,1536]{1,0:T(8,128)S(1)} %get-tuple-element.73), channel_id=1, source_target_pairs={{0,1},{1,0},{2,3},{3,2},{4,5},{5,4},{6,7},{7,6},{8,9},{9,8},{10,11... | collective-permute-start | bytes 4718600 | tf_op jit(solution)/shard_map/ppermute | solution.py:256
  (130 other events, 2011.6 us)

commit v2 on v1

--- a/solution.py
+++ b/solution.py
@@ -73,183 +73,503 @@
     )
 
 
-def experts_body(
-    rows_ref,
-    cot_ref,
-    hits_ref,
+def split_two(values):
+    lane = lax.broadcasted_iota(jnp.int32, values.shape, 1)
+    high = values.astype(jnp.bfloat16).astype(jnp.float32)
+    low = values - high
+    half_lanes = values.shape[1] // 2
+    moved = jnp.concatenate([low[:, half_lanes:], low[:, :half_lanes]], axis=1)
+    return jnp.where(lane < half_lanes, high, moved).astype(jnp.bfloat16)
+
+
+def block_order(me, count, turn):
+    left, right = me, count - 1 - me
+    near = jnp.minimum(left, right)
+    sign = jnp.where(left <= right, -1, 1)
+    paired = turn <= 2 * near
+    distance = jnp.where(paired, (turn + 1) // 2, turn - near)
+    toward = jnp.where(paired & (turn % 2 == 1), sign, -sign)
+    return me + toward * distance
+
+
+def expert_kernel(
+    owners,
+    local,
+    chunks,
+    rows_hbm,
+    cot_hbm,
     router_ref,
+    gateup_hbm,
+    down_hbm,
+    parts_hbm,
+    comb_hbm,
+    gates_out,
+    gateup_grad_hbm,
+    down_grad_hbm,
+    act_hbm,
+    hidden_hbm,
+    rows_all,
+    cot_all,
     gateup_ref,
     down_ref,
-    comb_ref,
-    grad_ref,
-    act_ref,
-    hidden_ref,
     gates_ref,
-    comb_sum,
-    grad_sum,
-    dot_sum,
+    send_grad,
+    send_comb,
+    recv_grad,
+    recv_comb,
+    load_sem,
+    weight_sem,
+    chain_send,
+    chain_recv,
+    swap_send,
+    swap_recv,
+    sums_send,
+    grad_recv,
+    comb_recv,
+    back_send,
+    back_recv,
+    comb_sem,
+    stage_sem,
 ):
-    step = pl.program_id(0)
-    steps = pl.num_programs(0)
-    hidden_units = down_ref.shape[1]
-    feat_width = rows_ref.shape[1]
-    number = lax.axis_index("expert") * steps + step
-    lane = lax.broadcasted_iota(jnp.int32, hits_ref.shape, 1)
-
-    @pl.when(step == 0)
-    def _():
-        hits = hits_ref[...] > 0
-        logits = jnp.dot(rows_ref[...], router_ref[...], preferred_element_type=jnp.float32)
-        logits = jnp.where(hits, logits, NEGATIVE)
-        raised = jnp.where(hits, jnp.exp(logits - jnp.max(logits, axis=1, keepdims=True)), 0.0)
-        gates_ref[...] = raised / jnp.sum(raised, axis=1, keepdims=True)
-
-    rows = rows_ref[...]
-    gate_part = jnp.dot(rows, gateup_ref[0, 0], preferred_element_type=jnp.float32)
-    up_part = jnp.dot(rows, gateup_ref[0, 1], preferred_element_type=jnp.float32)
-    raw = contract(cot_ref[...], down_ref[0], 1, 1)
-    here = lane == number
-    weight = jnp.sum(jnp.where(here, gates_ref[...], 0.0), axis=1, keepdims=True)
-    sigmoid_gate = jax.nn.sigmoid(gate_part)
-    silu_gate = gate_part * sigmoid_gate
-    activation = silu_gate * up_part
-    dots = jnp.where(here, jnp.sum(activation * raw, axis=1, keepdims=True), 0.0)
-    weighted = (activation * weight).astype(jnp.bfloat16)
-    act_ref[...] = weighted
-    grad_act = raw * (RESIDUAL * weight)
-    grad_gatepart = (
-        grad_act * up_part * (sigmoid_gate * (1.0 + gate_part * (1.0 - sigmoid_gate)))
-    ).astype(jnp.bfloat16)
-    grad_uppart = (grad_act * silu_gate).astype(jnp.bfloat16)
-    hidden_ref[:, :hidden_units] = grad_gatepart
-    hidden_ref[:, hidden_units:] = grad_uppart
-    comb = jnp.dot(weighted, down_ref[0], preferred_element_type=jnp.float32)
-    grad = contract(grad_gatepart, gateup_ref[0, 0], 1, 1) + contract(
-        grad_uppart, gateup_ref[0, 1], 1, 1
-    )
-
-    @pl.when(step == 0)
-    def _():
-        comb_sum[...] = comb
-        grad_sum[...] = grad
-        dot_sum[...] = dots
-
-    @pl.when(step > 0)
-    def _():
-        comb_sum[...] += comb
-        grad_sum[...] += grad
-        dot_sum[...] += dots
-
-    @pl.when(step == steps - 1)
-    def _():
-        comb_ref[...] = comb_sum[...].astype(jnp.bfloat16)
-        grad_ref[:, :feat_width] = grad_sum[...].astype(jnp.bfloat16)
-        grad_ref[:, feat_width:] = split_two(dot_sum[...])
-
-
-def split_two(values):
-    lane = lax.broadcasted_iota(jnp.int32, values.shape, 1)
-    high = values.astype(jnp.bfloat16)
-    low = values - high.astype(jnp.float32)
-    half_lanes = values.shape[1] // 2
-    moved = jnp.concatenate([low[:, half_lanes:], low[:, :half_lanes]], axis=1)
-    return jnp.where(lane < half_lanes, high.astype(jnp.float32), moved).astype(jnp.bfloat16)
-
-
-def experts(rows, cot, hits, router, gateup, down):
-    count, feat_width = rows.shape
-    local = gateup.shape[0]
-    units = down.shape[1]
-    lanes = hits.shape[1]
-    whole = lambda step: (0, 0)
-    return pl.pallas_call(
-        experts_body,
+    me = lax.axis_index("expert")
+    core = lax.axis_index("tensor")
+    sibling = {"tensor": 1 - core}
+    total, feat_width = rows_all.shape[1], rows_all.shape[2]
+    half = total // 2
+    units = down_ref.shape[1]
+    lanes = gates_ref.shape[1]
+    mine = pl.ds(pl.multiple_of(core * half, half), half)
+    others = pl.ds(pl.multiple_of((1 - core) * half, half), half)
+
+    barrier = pltpu.get_barrier_semaphore()
+    pl.semaphore_signal(barrier, inc=1, device_id=sibling, device_id_type=pl.DeviceIdType.MESH)
+    for shift in range(1, owners):
+        pl.semaphore_signal(
+            barrier,
+            inc=1,
+            device_id={"expert": lax.rem(me + shift, owners)},
+            device_id_type=pl.DeviceIdType.MESH,
+        )
+
+    def remote(src, dst, send, recv, device):
+        return pltpu.make_async_remote_copy(
+            src_ref=src,
+            dst_ref=dst,
+            send_sem=send,
+            recv_sem=recv,
+            device_id=device,
+            device_id_type=pl.DeviceIdType.MESH,
+        )
+
+    own_rows = pltpu.make_async_copy(rows_hbm, rows_all.at[me, mine], load_sem.at[0])
+    own_cot = pltpu.make_async_copy(cot_hbm, cot_all.at[me], load_sem.at[1])
+    own_rows.start()
+    own_cot.start()
+    for expert in range(local):
+        pltpu.make_async_copy(
+            gateup_hbm.at[expert], gateup_ref.at[expert], weight_sem.at[0, expert]
+        ).start()
+        pltpu.make_async_copy(
+            down_hbm.at[expert], down_ref.at[expert], weight_sem.at[1, expert]
+        ).start()
+    pl.semaphore_wait(barrier, owners)
+    own_rows.wait()
+    own_cot.wait()
+
+    buffers = (rows_all, cot_all)
+
+    def chain(step, what, side):
+        block = me - side * (step - 1)
+        to = me + side
+        there = (block >= 0) & (block < owners) & (to >= 0) & (to < owners)
+        safe = jnp.clip(block, 0, owners - 1)
+        at = 0 if side == 1 else 1
+        copy = remote(
+            buffers[what].at[safe, mine],
+            buffers[what].at[safe, mine],
+            chain_send.at[what, step - 1, at],
+            chain_recv.at[what, safe],
+            {"expert": jnp.clip(to, 0, owners - 1)},
+        )
+        return there, copy
+
+    def swap(what, block):
+        return remote(
+            buffers[what].at[block, mine],
+            buffers[what].at[block, mine],
+            swap_send.at[what, block],
+            swap_recv.at[what, block],
+            sibling,
+        )
+
+    def swap_arrival(what, block):
+        return remote(
+            buffers[what].at[block, others],
+            buffers[what].at[block, others],
+            swap_send.at[what, block],
+            swap_recv.at[what, block],
+            sibling,
+        )
+
+    def send_step(step):
+        for what in range(2):
+            for side in (1, -1):
+                there, copy = chain(step, what, side)
+
+                @pl.when(there)
+                def _():
+                    copy.start()
+
+    def arrivals(step):
+        for what in range(2):
+            for side in (1, -1):
+                block = me - side * step
+                there = (block >= 0) & (block < owners)
+                safe = jnp.clip(block, 0, owners - 1)
+
+                @pl.when(there)
+                def _():
+                    chain_copy = remote(
+                        buffers[what].at[safe, mine],
+                        buffers[what].at[safe, mine],
+                        chain_send.at[what, step - 1, 0],
+                        chain_recv.at[what, safe],
+                        sibling,
+                    )
+                    chain_copy.wait_recv()
+                    swap(what, safe).start()
+
+    swap(0, me).start()
+    send_step(1)
+
+    def expert_phase(comb_sum, grad_sum, dot_sum, hold_comb, hold_grad, hold_dot, act_stage, hidden_stage):
+        lane = lax.broadcasted_iota(jnp.int32, (total, lanes), 1)
+
+        def stage_copies(slot, expert, block):
+            return (
+                pltpu.make_async_copy(
+                    act_stage.at[slot], act_hbm.at[expert, block], stage_sem.at[0, slot]
+                ),
+                pltpu.make_async_copy(
+                    hidden_stage.at[slot], hidden_hbm.at[expert, block], stage_sem.at[1, slot]
+                ),
+            )
+
+        def sums_copies(turn):
+            return (
+                remote(send_grad, recv_grad.at[turn], sums_send.at[0], grad_recv.at[turn], sibling),
+                remote(send_comb, recv_comb.at[turn], sums_send.at[1], comb_recv.at[turn], sibling),
+            )
+
+        def back_copy(turn, block):
+            return remote(
+                recv_grad.at[turn],
+                parts_hbm.at[me],
+                back_send.at[turn],
+                back_recv.at[me],
+                {"expert": block},
+            )
+
+        def own_back():
+            return pltpu.make_async_copy(recv_grad.at[0], parts_hbm.at[me], back_send.at[0])
+
+        def comb_copy(turn, block):
+            return pltpu.make_async_copy(
+                recv_comb.at[turn],
+                comb_hbm.at[lax.rem(block - me + owners, owners)],
+                comb_sem.at[turn],
+            )
+
+        def settle(turn):
+            block = block_order(me, owners, turn)
+            copy_grad, copy_comb = sums_copies(turn)
+            copy_grad.wait_recv()
+            got = recv_grad[turn].astype(jnp.float32)
+            recv_grad[turn, :, :feat_width] = (hold_grad[...] + got[:, :feat_width]).astype(
+                jnp.bfloat16
+            )
+            dots = hold_dot[...] + got[:, feat_width:]
+            lower = lanes // 2
+            dots = dots + jnp.concatenate([dots[:, lower:], dots[:, :lower]], axis=1)
+            low_lane = lax.broadcasted_iota(jnp.int32, (half, lanes), 1) < lower
+            recv_grad[turn, :, feat_width:] = split_two(jnp.where(low_lane, dots, 0.0))
+
+            @pl.when(turn > 0)
+            def _():
+                back_copy(turn, block).start()
+
+            @pl.when(turn == 0)
+            def _():
+                own_back().start()
+
+            copy_comb.wait_recv()
+            recv_comb[turn] = (hold_comb[...] + recv_comb[turn].astype(jnp.float32)).astype(
+                jnp.bfloat16
+            )
+            comb_copy(turn, block).start()
+
+        def body(number, carry):
+            turn = number // local
+            expert = number % local
+            block = block_order(me, owners, turn)
+            slot = number % 2
+
+            @pl.when(expert == 0)
+            def _():
+                swap_arrival_needed = turn > 0
+
+                @pl.when(swap_arrival_needed)
+                def _():
+                    swap_arrival(1, block).wait_recv()
+
+                swap_arrival(0, block).wait_recv()
+                hits = cot_all[block, :, feat_width:].astype(jnp.float32) > 0.5
+                logits = jnp.dot(
+                    rows_all[block], router_ref[...], preferred_element_type=jnp.float32
+                )
+                logits = jnp.where(hits, logits, NEGATIVE)
+                raised = jnp.where(
+                    hits, jnp.exp(logits - jnp.max(logits, axis=1, keepdims=True)), 0.0
+                )
+                gates_ref[...] = raised / jnp.sum(raised, axis=1, keepdims=True)
+
+                @pl.when(turn == 0)
+                def _():
+                    gates_out[...] = gates_ref[mine]
+
+            @pl.when(number < local)
+            def _():
+                pltpu.make_async_copy(
+                    gateup_hbm.at[expert], gateup_ref.at[expert], weight_sem.at[0, expert]
+                ).wait()
+                pltpu.make_async_copy(
+                    down_hbm.at[expert], down_ref.at[expert], weight_sem.at[1, expert]
+                ).wait()
+
+            @pl.when(number >= 2)
+            def _():
+                for copy in stage_copies(slot, expert, block):
+                    copy.wait()
+
+            rows = rows_all[block]
+            gate_weight, up_weight, down = (
+                gateup_ref[expert, 0],
+                gateup_ref[expert, 1],
+                down_ref[expert],
+            )
+            gate_part = jnp.dot(rows, gate_weight, preferred_element_type=jnp.float32)
+            up_part = jnp.dot(rows, up_weight, preferred_element_type=jnp.float32)
+            raw = contract(cot_all[block, :, :feat_width], down, 1, 1)
+            here = lane == me * local + expert
+            weight = jnp.sum(jnp.where(here, gates_ref[...], 0.0), axis=1, keepdims=True)
+            sigmoid_gate = jax.nn.sigmoid(gate_part)
+            silu_gate = gate_part * sigmoid_gate
+            activation = silu_gate * up_part
+            dots = jnp.where(here, jnp.sum(activation * raw, axis=1, keepdims=True), 0.0)
+            weighted = (activation * weight).astype(jnp.bfloat16)
+            act_stage[slot] = weighted
+            grad_act = raw * (RESIDUAL * weight)
+            grad_gatepart = (
+                grad_act * up_part * (sigmoid_gate * (1.0 + gate_part * (1.0 - sigmoid_gate)))
+            ).astype(jnp.bfloat16)
+            grad_uppart = (grad_act * silu_gate).astype(jnp.bfloat16)
+            hidden_stage[slot, :, :units] = grad_gatepart
+            hidden_stage[slot, :, units:] = grad_uppart
+            for copy in stage_copies(slot, expert, block):
+                copy.start()
+            comb = jnp.dot(weighted, down, preferred_element_type=jnp.float32)
+            grad = contract(grad_gatepart, gate_weight, 1, 1) + contract(
+                grad_uppart, up_weight, 1, 1
+            )
+
+            @pl.when(expert == 0)
+            def _():
+                comb_sum[...] = comb
+                grad_sum[...] = grad
+                dot_sum[...] = dots
+
+            @pl.when(expert > 0)
+            def _():
+                comb_sum[...] += comb
+                grad_sum[...] += grad
+                dot_sum[...] += dots
+
+            @pl.when((expert == 1) & (turn > 0))
+            def _():
+                settle(turn - 1)
+
+            for step in range(1, owners):
+
+                @pl.when(number == step * local - 2)
+                def _():
+                    arrivals(step)
+                    if step + 1 < owners:
+                        send_step(step + 1)
+
+            @pl.when(expert == local - 1)
+            def _():
+                @pl.when(turn > 0)
+                def _():
+                    for copy in sums_copies(turn):
+                        copy.wait_send()
+
+                send_grad[:, :feat_width] = grad_sum[others].astype(jnp.bfloat16)
+                send_grad[:, feat_width:] = split_two(dot_sum[others])
+                send_comb[...] = comb_sum[others].astype(jnp.bfloat16)
+                for copy in sums_copies(turn):
+                    copy.start()
+                hold_grad[...] = grad_sum[mine]
+                hold_comb[...] = comb_sum[mine]
+                hold_dot[...] = dot_sum[mine]
+
+            return carry
+
+        lax.fori_loop(0, owners * local, body, 0)
+        settle(owners - 1)
+        for copy in sums_copies(owners - 1):
+            copy.wait_send()
+        for slot in range(2):
+            for copy in stage_copies(slot, 0, 0):
+                copy.wait()
+        for turn in range(owners):
+            block = block_order(me, owners, turn)
+            comb_copy(turn, block).wait()
+
+    pl.run_scoped(
+        expert_phase,
+        pltpu.VMEM((total, feat_width), jnp.float32),
+        pltpu.VMEM((total, feat_width), jnp.float32),
+        pltpu.VMEM((total, lanes), jnp.float32),
+        pltpu.VMEM((half, feat_width), jnp.float32),
+        pltpu.VMEM((half, feat_width), jnp.float32),
+        pltpu.VMEM((half, lanes), jnp.float32),
+        pltpu.VMEM((2, total, units), jnp.bfloat16),
+        pltpu.VMEM((2, total, 2 * units), jnp.bfloat16),
+    )
+
+    width = feat_width // chunks
+
+    def weights_body(act_ref, hidden_ref, gateup_out, down_out):
+        up_sum = sum(contract(rows_all[b], hidden_ref[0, b], 0, 0) for b in range(owners))
+        up_sum = up_sum.astype(jnp.bfloat16)
+        for chunk in range(chunks):
+            for part in range(2):
+                gateup_out[chunk, 0, part] = up_sum[
+                    chunk * width : (chunk + 1) * width, part * units : (part + 1) * units
+                ]
+        down_sum = sum(
+            contract(act_ref[0, b], cot_all[b, :, :feat_width], 0, 0) for b in range(owners)
+        )
+        down_sum = (RESIDUAL * down_sum).astype(jnp.bfloat16)
+        for chunk in range(chunks):
+            down_out[chunk, 0] = down_sum[:, chunk * width : (chunk + 1) * width]
+
+    pltpu.emit_pipeline(
+        weights_body,
         grid=(local,),
         in_specs=[
-            pl.BlockSpec((count, feat_width), whole),
-            pl.BlockSpec((count, feat_width), whole),
-            pl.BlockSpec((count, lanes), whole),
-            pl.BlockSpec((feat_width, lanes), whole),
-            pl.BlockSpec((1, 2, feat_width, units), lambda step: (step, 0, 0, 0)),
-            pl.BlockSpec((1, units, feat_width), lambda step: (step, 0, 0)),
+            pl.BlockSpec((1, owners, total, units), lambda e: (e, 0, 0, 0)),
+            pl.BlockSpec((1, owners, total, 2 * units), lambda e: (e, 0, 0, 0)),
         ],
         out_specs=[
-            pl.BlockSpec((count, feat_width), whole),
-            pl.BlockSpec((count, feat_width + lanes), whole),
-            pl.BlockSpec((count, units), lambda step: (0, step)),
-            pl.BlockSpec((count, 2 * units), lambda step: (0, step)),
-            pl.BlockSpec((count, lanes), whole),
+            pl.BlockSpec((chunks, 1, 2, width, units), lambda e: (0, e, 0, 0, 0)),
+            pl.BlockSpec((chunks, 1, units, width), lambda e: (0, e, 0, 0)),
         ],
+    )(act_hbm, hidden_hbm, gateup_grad_hbm, down_grad_hbm)
+
+    swap(0, me).wait_send()
+    for step in range(1, owners):
+        for what in range(2):
+            for side in (1, -1):
+                there, copy = chain(step, what, side)
+
+                @pl.when(there)
+                def _():
+                    copy.wait_send()
+
+                block = me - side * step
+                arrived = (block >= 0) & (block < owners)
+                safe = jnp.clip(block, 0, owners - 1)
+
+                @pl.when(arrived)
+                def _():
+                    swap(what, safe).wait_send()
+
+    pltpu.make_async_copy(recv_grad.at[0], parts_hbm.at[me], back_send.at[0]).wait()
+    for turn in range(1, owners):
+        block = block_order(me, owners, turn)
+        remote(
+            recv_grad.at[turn],
+            parts_hbm.at[me],
+            back_send.at[turn],
+            back_recv.at[me],
+            {"expert": block},
+        ).wait_send()
+        source = lax.rem(me + turn, owners)
+        remote(
+            recv_grad.at[turn],
+            parts_hbm.at[source],
+            back_send.at[turn],
+            back_recv.at[source],
+            {"expert": source},
+        ).wait_recv()
+
+
+def experts(rows, cot, router, gateup, down, owners, chunks):
+    half, feat_width = rows.shape
+    total = 2 * half
+    local, units = down.shape[0], down.shape[1]
+    lanes = router.shape[1]
+    wide = feat_width + lanes
+    any_space = pl.BlockSpec(memory_space=pl.ANY)
+    in_vmem = pl.BlockSpec(memory_space=pltpu.VMEM)
+    bf16 = jnp.bfloat16
+    return pl.pallas_call(
+        functools.partial(expert_kernel, owners, local, chunks),
+        in_specs=[any_space, any_space, in_vmem, any_space, any_space],
+        out_specs=[any_space, any_space, in_vmem, any_space, any_space, any_space, any_space],
         out_shape=[
-            jax.ShapeDtypeStruct((count, feat_width), jnp.bfloat16),
-            jax.ShapeDtypeStruct((count, feat_width + lanes), jnp.bfloat16),
-            jax.ShapeDtypeStruct((count, local * units), jnp.bfloat16),
-            jax.ShapeDtypeStruct((count, local * 2 * units), jnp.bfloat16),
-            jax.ShapeDtypeStruct((count, lanes), jnp.float32),
+            jax.ShapeDtypeStruct((owners, half, wide), bf16),
+            jax.ShapeDtypeStruct((owners, half, feat_width), bf16),
+            jax.ShapeDtypeStruct((half, lanes), jnp.float32),
+            jax.ShapeDtypeStruct((chunks, local, 2, feat_width // chunks, units), bf16),
+            jax.ShapeDtypeStruct((chunks, local, units, feat_width // chunks), bf16),
+            jax.ShapeDtypeStruct((local, owners, total, units), bf16),
+            jax.ShapeDtypeStruct((local, owners, total, 2 * units), bf16),
         ],
         scratch_shapes=[
-            pltpu.VMEM((count, feat_width), jnp.float32),
-            pltpu.VMEM((count, feat_width), jnp.float32),
-            pltpu.VMEM((count, lanes), jnp.float32),
+            pltpu.VMEM((owners, total, feat_width), bf16),
+            pltpu.VMEM((owners, total, wide), bf16),
+            pltpu.VMEM((local, 2, feat_width, units), bf16),
+            pltpu.VMEM((local, units, feat_width), bf16),
+            pltpu.VMEM((total, lanes), jnp.float32),
+            pltpu.VMEM((half, wide), bf16),
+            pltpu.VMEM((half, feat_width), bf16),
+            pltpu.VMEM((owners, half, wide), bf16),
+            pltpu.VMEM((owners, half, feat_width), bf16),
+            pltpu.SemaphoreType.DMA((2,)),
+            pltpu.SemaphoreType.DMA((2, local)),
+            pltpu.SemaphoreType.DMA((2, owners - 1, 2)),
+            pltpu.SemaphoreType.DMA((2, owners)),
+            pltpu.SemaphoreType.DMA((2, owners)),
+            pltpu.SemaphoreType.DMA((2, owners)),
+            pltpu.SemaphoreType.DMA((2,)),
+            pltpu.SemaphoreType.DMA((owners,)),
+            pltpu.SemaphoreType.DMA((owners,)),
+            pltpu.SemaphoreType.DMA((owners,)),
+            pltpu.SemaphoreType.DMA((owners,)),
+            pltpu.SemaphoreType.DMA((owners,)),
+            pltpu.SemaphoreType.DMA((2, 2)),
         ],
-        compiler_params=pltpu.CompilerParams(vmem_limit_bytes=56 * 2**20),
+        compiler_params=pltpu.CompilerParams(
+            vmem_limit_bytes=60 * 2**20, collective_id=0, has_side_effects=True
+        ),
         cost_estimate=pl.CostEstimate(
-            flops=2 * count * feat_width * units * 6 * local,
-            bytes_accessed=2 * (gateup.size + down.size) + 10 * count * feat_width,
-            transcendentals=count * units * local,
+            flops=2 * owners * total * feat_width * units * 9 * local,
+            bytes_accessed=80 * 2**20,
+            transcendentals=owners * total * units * local,
         ),
-    )(rows, cot, hits, router, gateup, down)
-
-
-def weights_body(blocks, chunks, *refs):
-    rows_refs, cot_refs = refs[:blocks], refs[blocks : 2 * blocks]
-    act_refs, hidden_refs = refs[2 * blocks : 3 * blocks], refs[3 * blocks : 4 * blocks]
-    gateup_ref, down_ref = refs[4 * blocks :]
-    units = down_ref.shape[2]
-    width = down_ref.shape[3]
-    for part in range(2):
-        total = sum(
-            contract(rows_refs[b][...], hidden_refs[b][:, part * units : (part + 1) * units], 0, 0)
-            for b in range(blocks)
-        ).astype(jnp.bfloat16)
-        for chunk in range(chunks):
-            gateup_ref[chunk, 0, part] = total[chunk * width : (chunk + 1) * width]
-    total = RESIDUAL * sum(
-        contract(act_refs[b][...], cot_refs[b][...], 0, 0) for b in range(blocks)
-    )
-    total = total.astype(jnp.bfloat16)
-    for chunk in range(chunks):
-        down_ref[chunk, 0] = total[:, chunk * width : (chunk + 1) * width]
-
-
-def expert_weights(rows, cots, acts, hiddens, chunks, local):
-    blocks = len(rows)
-    count, feat_width = rows[0].shape
-    units = acts[0].shape[1] // local
-    width = feat_width // chunks
-    whole = lambda step: (0, 0)
-    part = lambda step: (0, step)
-    return pl.pallas_call(
-        functools.partial(weights_body, blocks, chunks),
-        grid=(local,),
-        in_specs=[pl.BlockSpec((count, feat_width), whole)] * (2 * blocks)
-        + [pl.BlockSpec((count, units), part)] * blocks
-        + [pl.BlockSpec((count, 2 * units), part)] * blocks,
-        out_specs=[
-            pl.BlockSpec((chunks, 1, 2, width, units), lambda step: (0, step, 0, 0, 0)),
-            pl.BlockSpec((chunks, 1, units, width), lambda step: (0, step, 0, 0)),
-        ],
-        out_shape=[
-            jax.ShapeDtypeStruct((chunks, local, 2, width, units), jnp.bfloat16),
-            jax.ShapeDtypeStruct((chunks, local, units, width), jnp.bfloat16),
-        ],
-        compiler_params=pltpu.CompilerParams(vmem_limit_bytes=56 * 2**20),
-        cost_estimate=pl.CostEstimate(
-            flops=2 * blocks * count * feat_width * units * 3 * local,
-            bytes_accessed=4 * blocks * count * feat_width * 2 + 6 * local * units * feat_width,
-            transcendentals=0,
-        ),
-    )(*rows, *cots, *acts, *hiddens)
+    )(rows, cot, router, gateup, down)
 
 
 def swap_cores(values):
@@ -321,19 +641,11 @@
             jnp.concatenate([other, mine], axis=0),
         )
 
-    def both_cores(mine):
-        return jnp.concatenate([mine, swap_cores(mine)], axis=0)
-
-    cot_mine, cot_other = halves(out_grad)
-    cots = [jnp.concatenate([cot_mine, cot_other], axis=0)]
+    cot_mine, _ = halves(out_grad)
     hit_table = jnp.any(
         routes[:, :, None] == jnp.arange(lanes, dtype=jnp.int32)[None, None, :], axis=1
     ).astype(jnp.bfloat16)
-    hits_mine, hits_other = halves(hit_table)
-    hits = [jnp.concatenate([hits_mine, hits_other], axis=0)]
-    for slot in range(1, owners):
-        cots.append(both_cores(send_along(cot_mine, -slot)))
-        hits.append(both_cores(send_along(hits_mine, -slot)))
+    cot_wide = jnp.concatenate([out_grad, hit_table], axis=1)
     router_wide = jnp.pad(router_weight, ((0, 0), (0, lanes - expert_count)))
 
     cosine, sine_table = rotary_tables(SEQUENCE_LENGTH)
@@ -379,47 +691,19 @@
     middle = inputs_mine + RESIDUAL * (part_mine + swap_cores(part_other))
     unit_second, rms_second = norm_forward(middle)
     expert_in = (unit_second * expert_gain).astype(jnp.bfloat16)
-    rows = [both_cores(expert_in)]
+
+    parts, combs, gates, gateup_grad, down_grad, _, _ = experts(
+        expert_in, cot_wide, router_wide, gateup_weight, down_weight, owners, chunks
+    )
+    comb_total = combs[0].astype(jnp.float32)
     for slot in range(1, owners):
-        rows.append(both_cores(send_along(expert_in, -slot)))
-
-    comb_total = jnp.zeros((half, feat_width), jnp.float32)
-    grad_total = jnp.zeros((half, feat_width), jnp.float32)
-    dots_total = jnp.zeros((half, lanes), jnp.float32)
-    acts, hiddens = [None] * owners, [None] * owners
-    gates = None
-    for slot in range(owners):
-        comb, grad, acts[slot], hiddens[slot], slot_gates = experts(
-            rows[slot], cots[slot], hits[slot], router_wide, gateup_weight, down_weight
-        )
-        if slot == 0:
-            gates = slot_gates[:half]
-        comb = comb[:half].astype(jnp.float32) + swap_cores(comb[half:]).astype(jnp.float32)
-        grad_other = swap_cores(grad[half:])
-        grad_sum = grad[:half, :feat_width].astype(jnp.float32) + grad_other[
-            :, :feat_width
-        ].astype(jnp.float32)
-        dots = grad[:half, feat_width:].astype(jnp.float32) + grad_other[:, feat_width:].astype(
-            jnp.float32
-        )
-        if slot > 0:
-            comb = send_along(comb.astype(jnp.bfloat16), slot).astype(jnp.float32)
-            dots_whole = dots[:, : lanes // 2] + dots[:, lanes // 2 :]
-            dots_whole = jnp.pad(dots_whole, ((0, 0), (0, lanes // 2)))
-            back = send_along(
-                jnp.concatenate([grad_sum.astype(jnp.bfloat16), split_two(dots_whole)], axis=1),
-                slot,
-            )
-            grad_sum = back[:, :feat_width].astype(jnp.float32)
-            dots = back[:, feat_width:].astype(jnp.float32)
-        comb_total = comb_total + comb
-        grad_total = grad_total + grad_sum
-        dots_total = dots_total + dots
+        comb_total = comb_total + send_along(combs[slot], slot).astype(jnp.float32)
+    grad_total = jnp.sum(parts[:, :, :feat_width].astype(jnp.float32), axis=0)
+    dots_total = jnp.sum(parts[:, :, feat_width:].astype(jnp.float32), axis=0)
 
     mixed = (middle + RESIDUAL * comb_total).astype(jnp.bfloat16)
     output = in_order(mixed, swap_cores(mixed))
 
-    gateup_grad, down_grad = expert_weights(rows, cots, acts, hiddens, chunks, local_experts)
     dp_shape = (2,) * len(dp_bits)
     parts = []
     for part in range(2):

time: 685 us -> 567 us (0.83)
  starting transfers between devices: 163 us -> 35.2 us
  Pallas kernels: 125 us -> 189 us
  local copies, waits for them, and re-layouts: 69.1 us -> 34.8 us
  other arithmetic: 70.5 us -> 59.6 us
    ppermute x15 -> x3, starting transfers between devices: 108 us -> 6.84 us  [send_along(): lax.ppermute(values, 'expert', [(i, (i + shift) % count) for i in range(c...]
    ppermute x15 -> x3, waiting for transfers between devices: 75.4 us -> 0.01 us  [send_along(): lax.ppermute(values, 'expert', [(i, (i + shift) % count) for i in range(c...]
    ppermute x32, waiting for transfers between devices: 121 us -> 196 us  [halving(): got = lax.ppermute(send, axis, [(i, i ^ 1 << bit) for i in range(count)])]
    pallas_call x5 -> x1, Pallas kernels: 125 us -> 189 us  [experts(): pl.pallas_call(functools.partial(expert_kernel, owners, local, chunks), i...]
    ppermute x32, starting transfers between devices: 50.7 us -> 27.1 us  [halving(): got = lax.ppermute(send, axis, [(i, i ^ 1 << bit) for i in range(count)])]
    unnamed x188 -> x158, local copies, waits for them, and re-layouts: 23 us -> 9.64 us
    slice x11 -> x0, local copies, waits for them, and re-layouts: 8.39 us -> none  [the longest x4 5.2 us: per_device(): grad_other = swap_cores(grad[half:])]
  transfers between devices with their start and end apart: 72 -> 42, of which waited for: 30 -> 22; matrix products, arithmetic and copies ran while one was open for 25% -> 17% of each run, Pallas kernels for 19% -> 0%
where the time goes in v2:
time: 567 us; the launch traced here: 560 us
  waiting for transfers between devices  196 us (35%)
  Pallas kernels  189 us (33%)
  other arithmetic  59.6 us (11%)
  matrix products  43.8 us (8%)
  starting transfers between devices  35.2 us (6%)
  local copies, waits for them, and re-layouts  34.8 us (6%)
    ppermute x32, waiting for transfers between devices, halving(): got = lax.ppermute(send, axis, [(i, i ^ 1 << bit) for i in range(count)])  196 us
    pallas_call x1, Pallas kernels, experts(): pl.pallas_call(functools.partial(expert_kernel, owners, local, chunks), i...  189 us
    ppermute x32, starting transfers between devices, halving(): got = lax.ppermute(send, axis, [(i, i ^ 1 << bit) for i in range(count)])  27.1 us
    dot_general x1, matrix products, per_device(): jnp.einsum('sqjgd,skjd->sjgqk', grad_heads, value_rows, preferred_element...  11.9 us
  transfers between devices with their start and end apart: 42, of which 22 were waited for; matrix products, arithmetic and copies ran while one was open for 17% of the time, Pallas kernels for 0%

profile of v2, /device:TPU:0, one launch (start us, length us, event | category | flops | bytes accessed | tf_op | source)
XLA Modules:
  0.0 560.2 jit_solution(10839676260045650033)
XLA Ops:
  2.8 3.2 fusion.37
  9.7 3.1 fusion.5
  17.4 3.7 fusion.34
  22.1 3.1 fusion.90
  28.3 3.5 convert_element_type.381
  31.9 2.9 fusion.20
  36.5 2.8 pad_maximum_fusion.2.cot_hbm
  47.8 188.9 %shard_map.186 = (bf16[4,256,1664]{2,1,0:T(8,128)(2,1)}, bf16[4,256,1536]{2,1,0:T(8,128)(2,1)}, f32[256,128]{1,0:T(8,128)}, bf16[4,5,2,384,256]{4,3,2,1,0:T(8,12...) custom-call(bf16[256,1536]{1,0:T(8,128)(2,1)} %multiply_convert_fusion, ...), custom_call_target="tpu_custom_call" | custom-call | flops 72477573120 | bytes 83886080 | tf_op jit(solution)/shard_map/pallas_call | solution.py:527
  237.9 2.7 convert_reduce_fusion
  253.7 4.6 collective-permute-done.30
  259.8 2.7 multiply_convert_fusion.1
  270.6 36.8 %collective-permute-done.33 = f32[21,96]{1,0:T(8,128)S(1)} collective-permute-done((f32[21,96]{1,0:T(8,128)S(1)}, f32[21,96]{1,0:T(8,128)S(1)}, u32[]{:S(2)}, u32[]{:S(2)}) %collective-permute-start.33) | collective-permute-done | bytes 8096 | tf_op jit(solution)/shard_map/ppermute | solution.py:592
  313.3 11.9 %fusion = (f32[4,3,512]{2,1,0:T(4,128)S(1)}, f32[4,512,512,3]{2,1,3,0:T(8,128)}) fusion(f32[4,3,512]{2,1,0:T(4,128)S(1)} %fusion.4, f32[4,3,512]{2,1,0:T(4,128)S(1)} %copy-done.60, f32[4,512,512,3]{2,1,3,0:T(8,128)} %copy-done.2, pred[512,512]{0,1:T(8,128)(4,1)S(1)} %copy-done.31, bf16[512,4,64,1]{0,2,3,1:T(8,128)(2,1)} %bitcast.372, ...), kind=kOutput, calls=%fused_computation.3 | convolution fusion | flops 421521408 | bytes 26550272 | tf_op jit(solution)/shard_map/sqjgd,skjd->sjgqk/dot_general | solution.py:756
  326.2 7.0 %fusion.6 = bf16[4,3,512,512]{2,3,1,0:T(8,128)(2,1)S(1)} fusion(f32[4,512,512,3]{2,1,3,0:T(8,128)} %get-tuple-element.76, f32[4,3,512]{2,1,0:T(4,128)S(1)} %get-tuple-element.75, f32[4,3,512]{2,1,0:T(4,128)S(1)} %fusion.4, f32[4,3,512]{2,1,0:T(4,128)S(1)} %copy-done.60, f32[4,512,512,3]{2,1,3,0:T(8,128)S(1)} %bitcast.338, pred[512,512]{0,1:T(8,128)(4,1)S(1)} %copy-done.31), kind=kLoop, calls=%fused_computation.11 | loop fusion | flops 22020096 | bytes 31793152 | tf_op jit(solution)/shard_map/reshape.38
  336.5 3.6 fusion.45
  359.6 3.1 collective-permute-start.2
  362.9 5.5 collective-permute-done.25
  372.7 5.6 %collective-permute-done.39 = bf16[5,128,384]{2,1,0:T(8,128)(2,1)S(1)} collective-permute-done((bf16[5,128,384]{2,1,0:T(8,128)(2,1)S(1)}, bf16[5,128,384]{2,1,0:T(8,128)(2,1)S(1)}, u32[]{:S(2)}, u32[]{:S(2)}) %collective-permute-start.39) | collective-permute-done | bytes 491552 | tf_op jit(solution)/shard_map/ppermute | solution.py:592
  379.5 3.7 collective-permute-start.3
  384.7 30.2 %collective-permute-done.9 = f32[2,2,2,1,96]{4,2,1,0,3:T(2,128)S(1)} collective-permute-done((f32[2,2,2,1,96]{4,2,1,0,3:T(2,128)S(1)}, f32[2,2,2,1,96]{4,2,1,0,3:T(2,128)S(1)}, u32[]{:S(2)}, u32[]{:S(2)}) %collective-permute-start.9) | collective-permute-done | bytes 3104 | tf_op jit(solution)/shard_map/ppermute | solution.py:592
  416.5 3.1 collective-permute-done.10
  427.5 4.3 multiply_add_fusion
  433.8 59.5 %collective-permute-done.22 = bf16[2,2,96,384]{3,2,0,1:T(8,128)(2,1)S(1)} collective-permute-done((bf16[2,2,96,384]{3,2,0,1:T(8,128)(2,1)}, bf16[2,2,96,384]{3,2,0,1:T(8,128)(2,1)S(1)}, u32[]{:S(2)}, u32[]{:S(2)}) %collective-permute-start.22) | collective-permute-done | bytes 294944 | tf_op jit(solution)/shard_map/ppermute | solution.py:592
  494.1 6.0 %collective-permute-done.26 = bf16[2,2,96,384]{3,2,0,1:T(8,128)(2,1)S(1)} collective-permute-done((bf16[2,2,96,384]{3,2,0,1:T(8,128)(2,1)S(1)}, bf16[2,2,96,384]{3,2,0,1:T(8,128)(2,1)S(1)}, u32[]{:S(2)}, u32[]{:S(2)}) %collective-permute-start.26) | collective-permute-done | bytes 294944 | tf_op jit(solution)/shard_map/ppermute | solution.py:592
  501.7 5.2 collective-permute-done.23
  507.3 4.8 collective-permute-done.27
  512.9 5.1 collective-permute-done.24
  518.0 5.2 collective-permute-done.28
  529.7 5.0 collective-permute-done.18
  535.4 3.4 collective-permute-done.14
  542.8 2.8 collective-permute-done.19
  548.9 3.1 collective-permute-done.20
  (357 shorter events, 121.9 us)
Async XLA Ops:
  27.8 15.5 %collective-permute-start = (f32[256,1536]{1,0:T(8,128)}, f32[256,1536]{1,0:T(8,128)}, u32[]{:S(2)}, u32[]{:S(2)}) collective-permute-start(f32[256,1536]{1,0:T(8,128)} %constant_dynamic-slice_fusion.22), channel_id=1, source_target_pairs={{0,1},{1,0},{2,3},{3,2},{4,5},{5,4},{6,7},{7,6},{8,9},{9,8},{10,11... | collective-permute-start | bytes 4718600 | tf_op jit(solution)/shard_map/ppermute | solution.py:576
  242.4 112.4 %collective-permute-start.38 = (bf16[2,5,128,384]{3,2,1,0:T(8,128)(2,1)}, bf16[2,5,128,384]{3,2,1,0:T(8,128)(2,1)}, u32[]{:S(2)}, u32[]{:S(2)}) collective-permute-start(bf16[2,5,128,384]{3,2,1,0:T(8,128)(2,1)} %dynamic-slice_bitcast_fusion.3), channel_id=1, source_target_pairs={{0,16},{8,24},{16,0},{24,8},{1,17},{9,25},{17,1},{25,9},{2,18},{10... | collective-permute-start | bytes 2949128 | tf_op jit(solution)/shard_map/ppermute | solution.py:592
  245.0 112.9 %collective-permute-start.40 = (bf16[2,5,128,384]{3,2,1,0:T(8,128)(2,1)}, bf16[2,5,128,384]{3,2,1,0:T(8,128)(2,1)}, u32[]{:S(2)}, u32[]{:S(2)}) collective-permute-start(bf16[2,5,128,384]{3,2,1,0:T(8,128)(2,1)} %dynamic-slice_bitcast_fusion.2), channel_id=1, source_target_pairs={{0,8},{8,0},{16,24},{24,16},{1,9},{9,1},{17,25},{25,17},{2,10},{10... | collective-permute-start | bytes 2949128 | tf_op jit(solution)/shard_map/ppermute | solution.py:592
  252.8 271.8 %collective-permute-start.34 = (bf16[2,5,384,256]{3,2,1,0:T(8,128)(2,1)}, bf16[2,5,384,256]{3,2,1,0:T(8,128)(2,1)}, u32[]{:S(2)}, u32[]{:S(2)}) collective-permute-start(bf16[2,5,384,256]{3,2,1,0:T(8,128)(2,1)} %dynamic-slice_bitcast_fusion.1), channel_id=1, source_target_pairs={{0,16},{8,24},{16,0},{24,8},{1,17},{9,25},{17,1},{25,9},{2,18},{10... | collective-permute-start | bytes 5898248 | tf_op jit(solution)/shard_map/ppermute | solution.py:592
  262.5 46.0 %collective-permute-start.5 = (bf16[256,1536]{1,0:T(8,128)(2,1)S(1)}, bf16[256,1536]{1,0:T(8,128)(2,1)S(1)}, u32[]{:S(2)}, u32[]{:S(2)}) collective-permute-start(bf16[256,1536]{1,0:T(8,128)(2,1)S(1)} %multiply_convert_fusion.1), channel_id=1, source_target_pairs={{0,1},{1,0},{2,3},{3,2},{4,5},{5,4},{6,7},{7,6},{8,9},{9,8},{10,11... | collective-permute-start | bytes 2359304 | tf_op jit(solution)/shard_map/ppermute | solution.py:576
  267.9 39.6 %collective-permute-start.33 = (f32[21,96]{1,0:T(8,128)S(1)}, f32[21,96]{1,0:T(8,128)S(1)}, u32[]{:S(2)}, u32[]{:S(2)}) collective-permute-start(f32[21,96]{1,0:T(8,128)S(1)} %fusion.67), channel_id=1, source_target_pairs={{0,16},{8,24},{16,0},{24,8},{1,17},{9,25},{17,1},{25,9},{2,18},{10... | collective-permute-start | bytes 24200 | tf_op jit(solution)/shard_map/ppermute | solution.py:592
  307.4 117.3 %collective-permute-start.1 = (bf16[256,1536]{1,0:T(8,128)(2,1)}, bf16[256,1536]{1,0:T(8,128)(2,1)}, u32[]{:S(2)}, u32[]{:S(2)}) collective-permute-start(bf16[256,1536]{1,0:T(8,128)(2,1)} %get-tuple-element.34), channel_id=1, source_target_pairs={{0,2},{2,4},{4,6},{6,0},{1,3},{3,5},{5,7},{7,1},{8,10},{10,12},{12... | collective-permute-start | bytes 2359304 | tf_op jit(solution)/shard_map/ppermute | solution.py:581
  342.0 17.6 %collective-permute-start.21 = (bf16[2,2,2,96,384]{4,3,1,2,0:T(8,128)(2,1)S(1)}, bf16[2,2,2,96,384]{4,3,1,2,0:T(8,128)(2,1)S(1)}, u32[]{:S(2)}, u32[]{:S(2)}) collective-permute-start(bf16[2,2,2,96,384]{4,3,1,2,0:T(8,128)(2,1)S(1)} %bitcast.369), channel_id=1, source_target_pairs={{0,16},{8,24},{16,0},{24,8},{1,17},{9,25},{17,1},{25,9},{2,18},{10... | collective-permute-start | bytes 1769480 | tf_op jit(solution)/shard_map/ppermute | solution.py:592
  354.8 13.6 %collective-permute-start.25 = (bf16[2,2,2,96,384]{4,3,1,2,0:T(8,128)(2,1)S(1)}, bf16[2,2,2,96,384]{4,3,1,2,0:T(8,128)(2,1)S(1)}, u32[]{:S(2)}, u32[]{:S(2)}) collective-permute-start(bf16[2,2,2,96,384]{4,3,1,2,0:T(8,128)(2,1)S(1)} %bitcast.370), channel_id=1, source_target_pairs={{0,8},{8,0},{16,24},{24,16},{1,9},{9,1},{17,25},{25,17},{2,10},{10... | collective-permute-start | bytes 1769480 | tf_op jit(solution)/shard_map/ppermute | solution.py:592
  357.9 13.7 %collective-permute-start.6 = (bf16[256,1536]{1,0:T(8,128)(2,1)S(1)}, bf16[256,1536]{1,0:T(8,128)(2,1)S(1)}, u32[]{:S(2)}, u32[]{:S(2)}) collective-permute-start(bf16[256,1536]{1,0:T(8,128)(2,1)S(1)} %dynamic-slice_convert_fusion), channel_id=1, source_target_pairs={{0,1},{1,0},{2,3},{3,2},{4,5},{5,4},{6,7},{7,6},{8,9},{9,8},{10,11... | collective-permute-start | bytes 2359304 | tf_op jit(solution)/shard_map/ppermute | solution.py:576
  359.6 65.8 %collective-permute-start.2 = (bf16[256,1536]{1,0:T(8,128)(2,1)}, bf16[256,1536]{1,0:T(8,128)(2,1)}, u32[]{:S(2)}, u32[]{:S(2)}) collective-permute-start(bf16[256,1536]{1,0:T(8,128)(2,1)} %get-tuple-element.36), channel_id=1, source_target_pairs={{0,4},{2,6},{4,0},{6,2},{1,5},{3,7},{5,1},{7,3},{8,12},{10,14},{12... | collective-permute-start | bytes 2359304 | tf_op jit(solution)/shard_map/ppermute | solution.py:581
  368.4 10.0 %collective-permute-start.39 = (bf16[5,128,384]{2,1,0:T(8,128)(2,1)S(1)}, bf16[5,128,384]{2,1,0:T(8,128)(2,1)S(1)}, u32[]{:S(2)}, u32[]{:S(2)}) collective-permute-start(bf16[5,128,384]{2,1,0:T(8,128)(2,1)S(1)} %dynamic-slice_bitcast_fusion.7), channel_id=1, source_target_pairs={{0,8},{8,0},{16,24},{24,16},{1,9},{9,1},{17,25},{25,17},{2,10},{10... | collective-permute-start | bytes 1474568 | tf_op jit(solution)/shard_map/ppermute | solution.py:592
  371.6 11.8 %collective-permute-start.41 = (bf16[5,128,384]{2,1,0:T(8,128)(2,1)S(1)}, bf16[5,128,384]{2,1,0:T(8,128)(2,1)}, u32[]{:S(2)}, u32[]{:S(2)}) collective-permute-start(bf16[5,128,384]{2,1,0:T(8,128)(2,1)S(1)} %dynamic-slice_bitcast_fusion.6), channel_id=1, source_target_pairs={{0,16},{8,24},{16,0},{24,8},{1,17},{9,25},{17,1},{25,9},{2,18},{10... | collective-permute-start | bytes 1474568 | tf_op jit(solution)/shard_map/ppermute | solution.py:592
  379.5 47.4 %collective-permute-start.3 = (bf16[256,1536]{1,0:T(8,128)(2,1)}, bf16[256,1536]{1,0:T(8,128)(2,1)}, u32[]{:S(2)}, u32[]{:S(2)}) collective-permute-start(bf16[256,1536]{1,0:T(8,128)(2,1)} %get-tuple-element.35), channel_id=1, source_target_pairs={{0,6},{2,0},{4,2},{6,4},{1,7},{3,1},{5,3},{7,5},{8,14},{10,8},{12,... | collective-permute-start | bytes 2359304 | tf_op jit(solution)/shard_map/ppermute | solution.py:581
  383.4 31.6 %collective-permute-start.9 = (f32[2,2,2,1,96]{4,2,1,0,3:T(2,128)S(1)}, f32[2,2,2,1,96]{4,2,1,0,3:T(2,128)S(1)}, u32[]{:S(2)}, u32[]{:S(2)}) collective-permute-start(f32[2,2,2,1,96]{4,2,1,0,3:T(2,128)S(1)} %bitcast.380), channel_id=1, source_target_pairs={{0,2},{2,0},{4,6},{6,4},{1,3},{3,1},{5,7},{7,5},{8,10},{10,8},{12,... | collective-permute-start | bytes 9224 | tf_op jit(solution)/shard_map/ppermute | solution.py:592
  423.2 105.2 %collective-permute-start.36 = (bf16[2,5,384,256]{3,2,1,0:T(8,128)(2,1)}, bf16[2,5,384,256]{3,2,1,0:T(8,128)(2,1)S(1)}, u32[]{:S(2)}, u32[]{:S(2)}) collective-permute-start(bf16[2,5,384,256]{3,2,1,0:T(8,128)(2,1)} %dynamic-slice_bitcast_fusion), channel_id=1, source_target_pairs={{0,8},{8,0},{16,24},{24,16},{1,9},{9,1},{17,25},{25,17},{2,10},{10... | collective-permute-start | bytes 5898248 | tf_op jit(solution)/shard_map/ppermute | solution.py:592
  424.8 75.4 %collective-permute-start.17 = (bf16[2,2,2,96,640]{4,3,1,2,0:T(8,128)(2,1)S(1)}, bf16[2,2,2,96,640]{4,3,1,2,0:T(8,128)(2,1)S(1)}, u32[]{:S(2)}, u32[]{:S(2)}) collective-permute-start(bf16[2,2,2,96,640]{4,3,1,2,0:T(8,128)(2,1)S(1)} %bitcast.361), channel_id=1, source_target_pairs={{0,8},{8,0},{16,24},{24,16},{1,9},{9,1},{17,25},{25,17},{2,10},{10... | collective-permute-start | bytes 2949128 | tf_op jit(solution)/shard_map/ppermute | solution.py:592
  425.4 68.0 %collective-permute-start.22 = (bf16[2,2,96,384]{3,2,0,1:T(8,128)(2,1)}, bf16[2,2,96,384]{3,2,0,1:T(8,128)(2,1)S(1)}, u32[]{:S(2)}, u32[]{:S(2)}) collective-permute-start(bf16[2,2,96,384]{3,2,0,1:T(8,128)(2,1)} %dynamic-slice_bitcast_fusion.11), channel_id=1, source_target_pairs={{0,8},{8,0},{16,24},{24,16},{1,9},{9,1},{17,25},{25,17},{2,10},{10... | collective-permute-start | bytes 884744 | tf_op jit(solution)/shard_map/ppermute | solution.py:592
  431.8 69.3 %collective-permute-start.13 = (bf16[2,2,2,96,640]{4,3,1,2,0:T(8,128)(2,1)S(1)}, bf16[2,2,2,96,640]{4,3,1,2,0:T(8,128)(2,1)S(1)}, u32[]{:S(2)}, u32[]{:S(2)}) collective-permute-start(bf16[2,2,2,96,640]{4,3,1,2,0:T(8,128)(2,1)S(1)} %bitcast.360), channel_id=1, source_target_pairs={{0,16},{8,24},{16,0},{24,8},{1,17},{9,25},{17,1},{25,9},{2,18},{10... | collective-permute-start | bytes 2949128 | tf_op jit(solution)/shard_map/ppermute | solution.py:592
  493.4 6.7 %collective-permute-start.26 = (bf16[2,2,96,384]{3,2,0,1:T(8,128)(2,1)S(1)}, bf16[2,2,96,384]{3,2,0,1:T(8,128)(2,1)S(1)}, u32[]{:S(2)}, u32[]{:S(2)}) collective-permute-start(bf16[2,2,96,384]{3,2,0,1:T(8,128)(2,1)S(1)} %copy-done.56), channel_id=1, source_target_pairs={{0,16},{8,24},{16,0},{24,8},{1,17},{9,25},{17,1},{25,9},{2,18},{10... | collective-permute-start | bytes 884744 | tf_op jit(solution)/shard_map/ppermute | solution.py:592
  500.1 58.0 %collective-permute-start.7 = (f32[256,1536]{1,0:T(8,128)S(1)}, f32[256,1536]{1,0:T(8,128)S(1)}, u32[]{:S(2)}, u32[]{:S(2)}) collective-permute-start(f32[256,1536]{1,0:T(8,128)S(1)} %get-tuple-element.47), channel_id=1, source_target_pairs={{0,1},{1,0},{2,3},{3,2},{4,5},{5,4},{6,7},{7,6},{8,9},{9,8},{10,11... | collective-permute-start | bytes 4718600 | tf_op jit(solution)/shard_map/ppermute | solution.py:576
  500.2 38.7 %collective-permute-start.4 = (bf16[256,1536]{1,0:T(8,128)(2,1)S(1)}, bf16[256,1536]{1,0:T(8,128)(2,1)S(1)}, u32[]{:S(2)}, u32[]{:S(2)}) collective-permute-start(bf16[256,1536]{1,0:T(8,128)(2,1)S(1)} %get-tuple-element.48), channel_id=1, source_target_pairs={{0,1},{1,0},{2,3},{3,2},{4,5},{5,4},{6,7},{7,6},{8,9},{9,8},{10,11... | collective-permute-start | bytes 2359304 | tf_op jit(solution)/shard_map/ppermute | solution.py:576
  501.1 5.8 %collective-permute-start.23 = (bf16[2,96,384]{2,1,0:T(8,128)(2,1)S(1)}, bf16[2,96,384]{2,1,0:T(8,128)(2,1)S(1)}, u32[]{:S(2)}, u32[]{:S(2)}) collective-permute-start(bf16[2,96,384]{2,1,0:T(8,128)(2,1)S(1)} %dynamic-slice_bitcast_fusion.15), channel_id=1, source_target_pairs={{0,2},{2,0},{4,6},{6,4},{1,3},{3,1},{5,7},{7,5},{8,10},{10,8},{12,... | collective-permute-start | bytes 442376 | tf_op jit(solution)/shard_map/ppermute | solution.py:592
  512.1 5.9 %collective-permute-start.24 = (bf16[96,384]{1,0:T(8,128)(2,1)S(1)}, bf16[96,384]{1,0:T(8,128)(2,1)S(1)}, u32[]{:S(2)}, u32[]{:S(2)}) collective-permute-start(bf16[96,384]{1,0:T(8,128)(2,1)S(1)} %dynamic-slice_bitcast_fusion.19), channel_id=1, source_target_pairs={{0,4},{2,6},{4,0},{6,2},{1,5},{3,7},{5,1},{7,3},{8,12},{10,14},{12... | collective-permute-start | bytes 221192 | tf_op jit(solution)/shard_map/ppermute | solution.py:592
  523.2 11.4 %collective-permute-start.18 = (bf16[2,2,96,640]{3,2,0,1:T(8,128)(2,1)S(1)}, bf16[2,2,96,640]{3,2,0,1:T(8,128)(2,1)S(1)}, u32[]{:S(2)}, u32[]{:S(2)}) collective-permute-start(bf16[2,2,96,640]{3,2,0,1:T(8,128)(2,1)S(1)} %dynamic-slice_bitcast_fusion.8), channel_id=1, source_target_pairs={{0,16},{8,24},{16,0},{24,8},{1,17},{9,25},{17,1},{25,9},{2,18},{10... | collective-permute-start | bytes 1474568 | tf_op jit(solution)/shard_map/ppermute | solution.py:592
  524.6 14.2 %collective-permute-start.14 = (bf16[2,2,96,640]{3,2,0,1:T(8,128)(2,1)S(1)}, bf16[2,2,96,640]{3,2,0,1:T(8,128)(2,1)S(1)}, u32[]{:S(2)}, u32[]{:S(2)}) collective-permute-start(bf16[2,2,96,640]{3,2,0,1:T(8,128)(2,1)S(1)} %dynamic-slice_bitcast_fusion.9), channel_id=1, source_target_pairs={{0,8},{8,0},{16,24},{24,16},{1,9},{9,1},{17,25},{25,17},{2,10},{10... | collective-permute-start | bytes 1474568 | tf_op jit(solution)/shard_map/ppermute | solution.py:592
  528.4 27.0 %collective-permute-start.35 = (bf16[5,384,256]{2,1,0:T(8,128)(2,1)S(1)}, bf16[5,384,256]{2,1,0:T(8,128)(2,1)S(1)}, u32[]{:S(2)}, u32[]{:S(2)}) collective-permute-start(bf16[5,384,256]{2,1,0:T(8,128)(2,1)S(1)} %dynamic-slice_bitcast_fusion.5), channel_id=1, source_target_pairs={{0,8},{8,0},{16,24},{24,16},{1,9},{9,1},{17,25},{25,17},{2,10},{10... | collective-permute-start | bytes 2949128 | tf_op jit(solution)/shard_map/ppermute | solution.py:592
  534.6 21.0 %collective-permute-start.37 = (bf16[5,384,256]{2,1,0:T(8,128)(2,1)S(1)}, bf16[5,384,256]{2,1,0:T(8,128)(2,1)S(1)}, u32[]{:S(2)}, u32[]{:S(2)}) collective-permute-start(bf16[5,384,256]{2,1,0:T(8,128)(2,1)S(1)} %dynamic-slice_bitcast_fusion.4), channel_id=1, source_target_pairs={{0,16},{8,24},{16,0},{24,8},{1,17},{9,25},{17,1},{25,9},{2,18},{10... | collective-permute-start | bytes 2949128 | tf_op jit(solution)/shard_map/ppermute | solution.py:592
  538.7 6.9 %collective-permute-start.19 = (bf16[2,96,640]{2,1,0:T(8,128)(2,1)S(1)}, bf16[2,96,640]{2,1,0:T(8,128)(2,1)S(1)}, u32[]{:S(2)}, u32[]{:S(2)}) collective-permute-start(bf16[2,96,640]{2,1,0:T(8,128)(2,1)S(1)} %dynamic-slice_bitcast_fusion.12), channel_id=1, source_target_pairs={{0,2},{2,0},{4,6},{6,4},{1,3},{3,1},{5,7},{7,5},{8,10},{10,8},{12,... | collective-permute-start | bytes 737288 | tf_op jit(solution)/shard_map/ppermute | solution.py:592
  538.9 9.3 %collective-permute-start.15 = (bf16[2,96,640]{2,1,0:T(8,128)(2,1)S(1)}, bf16[2,96,640]{2,1,0:T(8,128)(2,1)S(1)}, u32[]{:S(2)}, u32[]{:S(2)}) collective-permute-start(bf16[2,96,640]{2,1,0:T(8,128)(2,1)S(1)} %dynamic-slice_bitcast_fusion.13), channel_id=1, source_target_pairs={{0,2},{2,0},{4,6},{6,4},{1,3},{3,1},{5,7},{7,5},{8,10},{10,8},{12,... | collective-permute-start | bytes 737288 | tf_op jit(solution)/shard_map/ppermute | solution.py:592
  545.7 6.3 %collective-permute-start.20 = (bf16[96,640]{1,0:T(8,128)(2,1)S(1)}, bf16[96,640]{1,0:T(8,128)(2,1)S(1)}, u32[]{:S(2)}, u32[]{:S(2)}) collective-permute-start(bf16[96,640]{1,0:T(8,128)(2,1)S(1)} %dynamic-slice_bitcast_fusion.16), channel_id=1, source_target_pairs={{0,4},{2,6},{4,0},{6,2},{1,5},{3,7},{5,1},{7,3},{8,12},{10,14},{12... | collective-permute-start | bytes 368648 | tf_op jit(solution)/shard_map/ppermute | solution.py:592
  548.4 6.3 %collective-permute-start.16 = (bf16[96,640]{1,0:T(8,128)(2,1)S(1)}, bf16[96,640]{1,0:T(8,128)(2,1)S(1)}, u32[]{:S(2)}, u32[]{:S(2)}) collective-permute-start(bf16[96,640]{1,0:T(8,128)(2,1)S(1)} %dynamic-slice_bitcast_fusion.17), channel_id=1, source_target_pairs={{0,4},{2,6},{4,0},{6,2},{1,5},{3,7},{5,1},{7,3},{8,12},{10,14},{12... | collective-permute-start | bytes 368648 | tf_op jit(solution)/shard_map/ppermute | solution.py:592
  (88 other events, 968.0 us)
